TPU v7x, 256 devices: a whole 4x4x8 slice. The times are simulated.
256 devices in a mesh: gz: 16 (over z, x_lo), gy: 16 (over x_hi, y, core).
Axes of the slice: x: 4 (x_hi: 2, x_lo: 2; x = x_hi * 2 + x_lo), y: 4, z: 8, core: 2. Of those that a mesh axis runs over, the one named last changes fastest.
Arguments:
- displacement: float32 [3, 256, 512, 256], P(None, 'gz', 'gy'), may hold values from -6 to 6
- design: float32 [256, 512, 256], P('gz', 'gy'), may hold values from 0.1 to 0.95
- void_mask: int32 [256, 512, 256], P('gz', 'gy'), may hold values 0 or 1
- solid_mask: int32 [256, 512, 256], P('gz', 'gy'), may hold values 0 or 1
- stiffness: float32 [24, 24], replicated, as said below
Outputs:
- new_design: float32 [256, 512, 256], P('gz', 'gy')
- sensitivity: float32 [256, 512, 256], P('gz', 'gy')
Inputs may be any that keep to these rules, and one draw needn't show every extreme that they name: stiffness is symmetric, and each diagonal entry exceeds the sum of magnitudes of the rest of its row.
All inputs are finite; a program needn't handle non-finite values. No bound on the sum of `void_mask` or of `solid_mask` on one device may be relied on, other than what follows from the above.
Results may differ from a plain program's by a relative error of at most 0.0001.
Values sent between devices are 32-bit elements; how exact they have to be, the bound alone decides.
A program may use at most 64 MiB of HBM per device.

v0:
```python
import jax
import jax.numpy as jnp
from jax import lax
from jax.sharding import PartitionSpec as P

ITERS = 8


TAP_TABLE = (1.0, 2.0, 3.0, 4.0, 3.0, 2.0, 1.0)
LOW_LOG = -25.0
HIGH_LOG = 25.0
MOVE_LIMIT = 0.2
VOLUME_FRACTION = 0.5
PENALTY = 3.0


def padded_2(block, sides, width):
    for axis, dim in sides:
        count = lax.axis_size(axis)
        forward = [(i, i + 1) for i in range(count - 1)]
        backward = [(target, source) for source, target in forward]
        low = lax.ppermute(
            lax.slice_in_dim(block, block.shape[dim] - width, None, axis=dim), axis, forward
        )
        high = lax.ppermute(lax.slice_in_dim(block, 0, width, axis=dim), axis, backward)
        block = jnp.concatenate([low, block, high], axis=dim)
    return block


def passed_along(block, axis, distance):
    devices = range(lax.axis_size(axis))
    route = [(i - distance, i) for i in devices if i - distance in devices]
    return lax.ppermute(block, axis, route)


def line_weights(position, extent):
    offsets = jnp.arange(-3, 4, dtype=jnp.int32)
    tap_values = jnp.asarray(TAP_TABLE, jnp.float32)

    def row_total(locations):
        nearby = locations[:, None] + offsets[None, :]
        inside = ((nearby >= 0) & (nearby < extent)).astype(jnp.float32)
        return jnp.sum(inside * tap_values[None, :], axis=1)

    totals = row_total(position)
    nearby = position[:, None] + offsets[None, :]
    inside = ((nearby >= 0) & (nearby < extent)).astype(jnp.float32)
    near_totals = row_total(nearby.reshape(-1)).reshape(nearby.shape)
    spread = jnp.sum(inside * tap_values[None, :] / near_totals, axis=1)
    return (totals, spread)


def pass_along(padded, dimension, extent):
    summed = TAP_TABLE[0] * lax.slice_in_dim(padded, 0, extent, axis=dimension)
    for tap_index in range(1, 7):
        summed = summed + TAP_TABLE[tap_index] * lax.slice_in_dim(
            padded, tap_index, tap_index + extent, axis=dimension
        )
    return summed


def energies(extended, stiffness, layer_count, row_count, col_count):

    def one_layer(layer):
        slab_pair = lax.dynamic_slice_in_dim(extended, layer, 2, 1)
        corners = []
        for step_z in range(2):
            for step_y in range(2):
                for step_x in range(2):
                    for component in range(3):
                        corners.append(
                            slab_pair[
                                component,
                                step_z,
                                step_y : step_y + row_count,
                                step_x : step_x + col_count,
                            ]
                        )
        stacked = jnp.stack(corners)
        forces = jnp.einsum("ab,byx->ayx", stiffness, stacked, precision=lax.Precision.HIGHEST)
        return jnp.sum(stacked * forces, axis=0)

    return lax.map(one_layer, jnp.arange(layer_count, dtype=jnp.int32))


def smooth(fields):
    stacked = jnp.stack(fields)
    layer_count, row_count, col_count = stacked.shape[1:]
    padded = padded_2(stacked, (("gz", 1), ("gy", 2)), 3)
    along_z = pass_along(padded, 1, layer_count)
    along_y = pass_along(along_z, 2, row_count)
    padded_x = jnp.pad(along_y, ((0, 0), (0, 0), (0, 0), (3, 3)))
    return pass_along(padded_x, 3, col_count)


def volumes(log_values, make_design, inverse_total):
    designs = [make_design(value) for value in log_values]
    filtered = smooth(tuple(designs))
    local_sums = jnp.sum(filtered * inverse_total[None], axis=(1, 2, 3))
    return lax.psum(local_sums, ("gz", "gy"))


def per_device(displacement, design, void_mask, solid_mask, stiffness):
    layer_count, row_count, col_count = design.shape
    top_layer = passed_along(displacement[:, :1], "gz", -1)
    extended = jnp.concatenate([displacement, top_layer], axis=1)
    side_row = passed_along(extended[:, :, :1], "gy", -1)
    extended = jnp.concatenate([extended, side_row], axis=2)
    extended = jnp.pad(extended, ((0, 0), (0, 0), (0, 0), (0, 1)))
    energy = energies(extended, stiffness, layer_count, row_count, col_count)
    full_layers = layer_count * lax.axis_size("gz")
    full_rows = row_count * lax.axis_size("gy")
    place_z = lax.axis_index("gz") * layer_count + jnp.arange(layer_count, dtype=jnp.int32)
    place_y = lax.axis_index("gy") * row_count + jnp.arange(row_count, dtype=jnp.int32)
    totals_z, spread_z = line_weights(place_z, full_layers)
    totals_y, spread_y = line_weights(place_y, full_rows)
    totals_x, spread_x = line_weights(jnp.arange(col_count, dtype=jnp.int32), col_count)
    inverse_total = 1.0 / (
        totals_z[:, None, None] * totals_y[None, :, None] * totals_x[None, None, :]
    )
    volume_weight = spread_z[:, None, None] * spread_y[None, :, None] * spread_x[None, None, :]
    physical = smooth((design,))[0] * inverse_total
    sensitivity = smooth((-PENALTY * physical * physical * energy * inverse_total,))[0]
    root = jnp.sqrt(-sensitivity / volume_weight)
    lower = jnp.maximum(design - MOVE_LIMIT, 0.0)
    upper = jnp.minimum(design + MOVE_LIMIT, 1.0)
    target = VOLUME_FRACTION * full_layers * full_rows * col_count

    def candidate(log_value):
        moved = jnp.clip(design * root * jnp.exp(-0.5 * log_value), lower, upper)
        return jnp.where(solid_mask == 1, 1.0, jnp.where(void_mask == 1, 0.0, moved))

    low_log = jnp.asarray(LOW_LOG, jnp.float32)
    high_log = jnp.asarray(HIGH_LOG, jnp.float32)
    end_volumes = volumes([low_log, high_log], candidate, inverse_total)
    low_volume = end_volumes[0]
    high_volume = end_volumes[1]
    for step in range(ITERS):
        middle = 0.5 * (low_log + high_log)
        middle_volume = volumes([middle], candidate, inverse_total)[0]
        above = middle_volume > target
        low_log = jnp.where(above, middle, low_log)
        low_volume = jnp.where(above, middle_volume, low_volume)
        high_log = jnp.where(above, high_log, middle)
        high_volume = jnp.where(above, high_volume, middle_volume)
    fraction = (low_volume - target) / (low_volume - high_volume)
    final = low_log + fraction * (high_log - low_log)
    return (candidate(final), sensitivity)


def solution(mesh):
    return jax.shard_map(
        per_device,
        mesh=mesh,
        in_specs=(
            P(None, "gz", "gy", None),
            P("gz", "gy", None),
            P("gz", "gy", None),
            P("gz", "gy", None),
            P(),
        ),
        out_specs=(P("gz", "gy", None), P("gz", "gy", None)),
        check_vma=False,
    )
```

profile of v0, /device:TPU:1, one launch (start us, length us, event | category | flops | bytes accessed | tf_op | source)
XLA Modules:
  0.0 1082.8 jit_solution(1921298818242245703)
XLA Ops:
  2.2 3.9 collective-permute-start
  27.3 155.6 %while.11 = (s32[]{:T(128)}, f32[16,32,256]{2,1,0:T(8,128)}, s32[16]{0:T(128)S(1)}, f32[3,17,33,257]{3,0,2,1:T(4,128)}, f32[24,24]{1,0:T(8,128)S(1)}) while((s32[]{:T(128)}, f32[16,32,256]{2,1,0:T(8,128)}, s32[16]{0:T(128)S(1)}, f32[3,17,33,257]{3,0,2,1:T(4,128)}, f32[24,24]{1,0:T(8,128)S(1)}) %tuple.87), condition=%wide.region_5.6_spmd.clone, body=%wide.region_3.5_spmd.sunk.clone | while | flops 57008136 | bytes 4033439 | solution.py:83
  30.0 4.7 dynamic-slice_bitcast_fusion.26
  40.0 4.3 dynamic-slice_bitcast_fusion.26
  49.6 4.6 dynamic-slice_bitcast_fusion.26
  59.6 4.2 dynamic-slice_bitcast_fusion.26
  69.2 4.1 dynamic-slice_bitcast_fusion.26
  78.7 4.1 dynamic-slice_bitcast_fusion.26
  88.1 4.6 dynamic-slice_bitcast_fusion.26
  98.1 4.5 dynamic-slice_bitcast_fusion.26
  108.0 4.6 dynamic-slice_bitcast_fusion.26
  117.9 4.2 dynamic-slice_bitcast_fusion.26
  127.5 4.1 dynamic-slice_bitcast_fusion.26
  136.9 4.7 dynamic-slice_bitcast_fusion.26
  146.9 4.2 dynamic-slice_bitcast_fusion.26
  156.5 4.1 dynamic-slice_bitcast_fusion.26
  165.9 4.7 dynamic-slice_bitcast_fusion.26
  176.0 4.3 dynamic-slice_bitcast_fusion.26
  186.5 4.4 collective-permute-start.6
  193.5 4.3 collective-permute-done.7
  203.3 3.9 collective-permute-done.9
  210.8 4.4 collective-permute-start.10
  216.8 3.7 collective-permute-done.11
  220.6 3.9 collective-permute-start.12
  232.6 94.0 %psum.63 = f32[]{:T(128)} all-reduce(f32[]{:T(128)} %fusion.246), channel_id=1, replica_groups=mesh['gz'=16,'gy'=16] {'gz','gy'}, use_global_device_ids=true, to_apply=%region_13.14 | all-reduce | flops 1 | bytes 8 | tf_op jit(solution)/shard_map/psum | solution.py:100
  331.3 3.7 collective-permute-done.15
  340.4 3.8 collective-permute-done.17
  346.5 82.9 %psum.64 = f32[]{:T(128)} all-reduce(f32[]{:T(128)} %fusion.245), channel_id=1, replica_groups=mesh['gz'=16,'gy'=16] {'gz','gy'}, use_global_device_ids=true, to_apply=%region_15.16 | all-reduce | flops 1 | bytes 8 | tf_op jit(solution)/shard_map/psum | solution.py:100
  433.2 3.7 collective-permute-done.19
  437.0 4.4 collective-permute-start.20
  443.4 3.9 collective-permute-done.21
  449.7 82.5 %psum.65 = f32[]{:T(128)} all-reduce(f32[]{:T(128)} %fusion.244), channel_id=1, replica_groups=mesh['gz'=16,'gy'=16] {'gz','gy'}, use_global_device_ids=true, to_apply=%region_17.18 | all-reduce | flops 1 | bytes 8 | tf_op jit(solution)/shard_map/psum | solution.py:100
  539.9 4.4 collective-permute-start.24
  546.3 3.9 collective-permute-done.25
  552.5 82.6 %psum.66 = f32[]{:T(128)} all-reduce(f32[]{:T(128)} %fusion.243), channel_id=1, replica_groups=mesh['gz'=16,'gy'=16] {'gz','gy'}, use_global_device_ids=true, to_apply=%region_19.20 | all-reduce | flops 1 | bytes 8 | tf_op jit(solution)/shard_map/psum | solution.py:100
  642.7 4.4 collective-permute-start.28
  655.3 82.5 %psum.67 = f32[]{:T(128)} all-reduce(f32[]{:T(128)} %fusion.242), channel_id=1, replica_groups=mesh['gz'=16,'gy'=16] {'gz','gy'}, use_global_device_ids=true, to_apply=%region_21.22 | all-reduce | flops 1 | bytes 8 | tf_op jit(solution)/shard_map/psum | solution.py:100
  745.5 4.4 collective-permute-start.32
  751.9 3.9 collective-permute-done.33
  758.2 82.5 %psum.68 = f32[]{:T(128)} all-reduce(f32[]{:T(128)} %fusion.241), channel_id=1, replica_groups=mesh['gz'=16,'gy'=16] {'gz','gy'}, use_global_device_ids=true, to_apply=%region_23.24 | all-reduce | flops 1 | bytes 8 | tf_op jit(solution)/shard_map/psum | solution.py:100
  848.3 4.4 collective-permute-start.36
  854.7 3.9 collective-permute-done.37
  860.9 82.5 %psum.69 = f32[]{:T(128)} all-reduce(f32[]{:T(128)} %fusion.240), channel_id=1, replica_groups=mesh['gz'=16,'gy'=16] {'gz','gy'}, use_global_device_ids=true, to_apply=%region_25.26 | all-reduce | flops 1 | bytes 8 | tf_op jit(solution)/shard_map/psum | solution.py:100
  947.3 3.7 collective-permute-done.39
  951.1 4.4 collective-permute-start.40
  963.0 5.3 collective-permute-done.42
  968.4 4.1 collective-permute-start.44
  982.6 86.4 %all-reduce.12 = (f32[]{:T(128)}, f32[2]{0:T(128)S(1)}) all-reduce(f32[]{:T(128)} %fusion.239, f32[2]{0:T(128)S(1)} %fusion.24), channel_id=1, replica_groups=mesh['gz'=16,'gy'=16] {'gz','gy'}, use_global_device_ids=true, to_apply=%region_27.28 | all-reduce | flops 3 | bytes 24 | tf_op jit(solution)/shard_map/psum | solution.py:100
  (246 shorter events, 189.5 us)
Async XLA Ops:
  2.2 16.8 %collective-permute-start = (f32[1,3,32,256]{3,2,1,0:T(8,128)}, f32[1,3,32,256]{3,2,1,0:T(8,128)S(1)}, u32[]{:S(2)}, u32[]{:S(2)}) collective-permute-start(f32[1,3,32,256]{3,2,1,0:T(8,128)} %get-tuple-element.121), channel_id=1, source_target_pairs={{0,16},{16,32},{32,48},{48,64},{64,80},{80,96},{96,112},{112,128},... | collective-permute-start | bytes 294920 | tf_op jit(solution)/shard_map/ppermute | solution.py:22
  6.2 12.9 %collective-permute-start.1 = (f32[1,3,32,256]{3,2,1,0:T(8,128)S(1)}, f32[1,3,32,256]{3,2,1,0:T(8,128)S(1)}, u32[]{:S(2)}, u32[]{:S(2)}) collective-permute-start(f32[1,3,32,256]{3,2,1,0:T(8,128)S(1)} %get-tuple-element.122), channel_id=1, source_target_pairs={{16,0},{32,16},{48,32},{64,48},{80,64},{96,80},{112,96},{128,112},... | collective-permute-start | bytes 294920 | tf_op jit(solution)/shard_map/ppermute | solution.py:25
  8.4 6.9 collective-permute-start.4
  9.8 9.3 copy-start
  15.4 9.4 collective-permute-start.5
  19.7 163.1 %collective-permute-start.2 = (f32[1,22,3,256]{3,2,1,0:T(4,128)}, f32[1,22,3,256]{3,2,1,0:T(4,128)}, u32[]{:S(2)}, u32[]{:S(2)}) collective-permute-start(f32[1,22,3,256]{3,2,1,0:T(4,128)} %get-tuple-element.101), channel_id=1, source_target_pairs={{0,1},{1,2},{2,3},{3,4},{4,5},{5,6},{6,7},{7,8},{8,9},{9,10},{10,1... | collective-permute-start | bytes 202760 | tf_op jit(solution)/shard_map/ppermute | solution.py:22
  22.8 4.4 copy-start.3
  22.9 160.0 %collective-permute-start.3 = (f32[1,22,3,256]{3,2,1,0:T(4,128)}, f32[1,22,3,256]{3,2,1,0:T(4,128)}, u32[]{:S(2)}, u32[]{:S(2)}) collective-permute-start(f32[1,22,3,256]{3,2,1,0:T(4,128)} %get-tuple-element.102), channel_id=1, source_target_pairs={{1,0},{2,1},{3,2},{4,3},{5,4},{6,5},{7,6},{8,7},{9,8},{10,9},{11,1... | collective-permute-start | bytes 202760 | tf_op jit(solution)/shard_map/ppermute | solution.py:25
  186.5 6.9 collective-permute-start.6
  191.0 6.8 collective-permute-start.7
  197.8 5.5 collective-permute-start.8
  201.4 5.8 collective-permute-start.9
  210.8 6.0 collective-permute-start.10
  215.2 5.4 collective-permute-start.11
  220.6 6.3 collective-permute-start.12
  224.5 5.8 collective-permute-start.13
  327.5 3.8 collective-permute-start.14
  329.7 5.4 collective-permute-start.15
  335.1 5.3 collective-permute-start.16
  338.4 5.8 collective-permute-start.17
  430.3 2.9 collective-permute-start.18
  431.6 5.4 collective-permute-start.19
  437.0 6.4 collective-permute-start.20
  441.5 5.8 collective-permute-start.21
  533.2 2.9 collective-permute-start.22
  534.5 5.4 collective-permute-start.23
  539.9 6.4 collective-permute-start.24
  544.3 5.8 collective-permute-start.25
  636.0 2.9 collective-permute-start.26
  637.3 5.4 collective-permute-start.27
  642.7 6.5 collective-permute-start.28
  647.1 5.8 collective-permute-start.29
  738.8 2.9 collective-permute-start.30
  740.1 5.4 collective-permute-start.31
  745.5 6.4 collective-permute-start.32
  750.0 5.8 collective-permute-start.33
  841.6 2.9 collective-permute-start.34
  842.9 5.4 collective-permute-start.35
  848.3 6.4 collective-permute-start.36
  852.8 5.8 collective-permute-start.37
  944.4 2.9 collective-permute-start.38
  945.7 5.4 collective-permute-start.39
  951.1 11.1 %collective-permute-start.40 = (f32[1,22,3,256]{3,2,1,0:T(4,128)S(1)}, f32[1,22,3,256]{3,2,1,0:T(4,128)S(1)}, u32[]{:S(2)}, u32[]{:S(2)}) collective-permute-start(f32[1,22,3,256]{3,2,1,0:T(4,128)S(1)} %get-tuple-element.83), channel_id=1, source_target_pairs={{0,1},{1,2},{2,3},{3,4},{4,5},{5,6},{6,7},{7,8},{8,9},{9,10},{10,1... | collective-permute-start | bytes 202760 | tf_op jit(solution)/shard_map/ppermute | solution.py:22
  955.6 6.7 collective-permute-start.41
  957.5 10.8 collective-permute-start.42
  961.0 7.4 collective-permute-start.43
  968.4 7.9 collective-permute-start.44
  972.5 6.8 collective-permute-start.45
  (3 other events, 5.1 us)
where the time goes:
time: 1090 us; the launch traced here: 1080 us
  blocking collectives  676 us (62%)
  local copies, waits for them, and re-layouts  116 us (11%)
  starting transfers between devices  112 us (10%)
  waiting for transfers between devices  78 us (7%)
  other arithmetic  35.2 us (3%)
  loops' own time  33.5 us (3%)
  between operations  18.7 us (2%)
  matrix products  13.2 us (1%)
    psum x8, blocking collectives, volumes(): return lax.psum(local_sums, ('gz', 'gy'))  676 us
    ppermute x22, starting transfers between devices, padded_2(): lax.ppermute(lax.slice_in_dim(block, block.shape[dim] - width, None, axis...  70.7 us
    squeeze x16, local copies, waits for them, and re-layouts, one_layer(): stacked = jnp.stack(corners)  69.8 us
    ppermute x22, waiting for transfers between devices, padded_2(): lax.ppermute(lax.slice_in_dim(block, 0, width, axis=dim), axis, backward)  67.9 us
    ppermute x22, starting transfers between devices, padded_2(): lax.ppermute(lax.slice_in_dim(block, 0, width, axis=dim), axis, backward)  36.3 us
    another operation x1, loops' own time, energies(): return lax.map(one_layer, jnp.arange(layer_count, dtype=jnp.int32))  33.5 us
  transfers between devices with their start and end apart: 46, of which 29 were waited for; matrix products, arithmetic and copies ran while one was open for 12% of the time, Pallas kernels for 0%

commit v1 on v0

v1 whole, which is shorter than its diff:
```python
import functools

import jax
import jax.numpy as jnp
from jax import lax
from jax.experimental import pallas as pl
from jax.experimental.pallas import tpu as pltpu
from jax.sharding import PartitionSpec as P

MESH = pl.DeviceIdType.MESH
F32 = jnp.float32
BF16 = jnp.bfloat16

TAPS = (1.0, 2.0, 3.0, 4.0, 3.0, 2.0, 1.0)
LOW_LOG = -25.0
HIGH_LOG = 25.0
MOVE_LIMIT = 0.2
VOLUME_FRACTION = 0.5
PENALTY = 3.0
SPLIT = 16

H = 3
Y0 = 8


def line_total(p, extent):
    low = jnp.maximum(3 - p, 0)
    high = jnp.maximum(p - (extent - 4), 0)
    missing = low * (low + 1) + high * (high + 1)
    return 16.0 - 0.5 * missing.astype(F32)


def line_spread(p, extent):
    total = None
    for d in range(-3, 4):
        near = p + d
        term = jnp.where(
            (near >= 0) & (near < extent), TAPS[d + 3] / line_total(near, extent), 0.0
        )
        total = term if total is None else total + term
    return total


def iota(shape, dim):
    return lax.broadcasted_iota(jnp.int32, shape, dim)


def split_bf16(x):
    high = x.astype(BF16)
    low = (x - high.astype(F32)).astype(BF16)
    return high, low


def dot(a, b):
    return jnp.dot(a, b, preferred_element_type=F32)


def row_filter(ref, layer, rows):
    c = [ref[layer, Y0 - H + t : Y0 - H + t + rows, :] for t in range(7)]
    return (c[0] + c[6]) + 2.0 * (c[1] + c[5]) + 3.0 * (c[2] + c[4]) + 4.0 * c[3]


def layer_filter(src, dst, layers):
    _, rows, cols = src.shape
    for r in range(0, rows, 8):
        for c in range(0, cols, 128):
            at = (slice(r, r + 8), slice(c, c + 128))
            f = [src[(k,) + at] for k in range(layers + 2 * H)]
            f = [a + b for a, b in zip(f, f[1:])]
            f = [a + b for a, b in zip(f, f[2:])]
            f = [a + b for a, b in zip(f, f[1:])]
            f = [a + b for a, b in zip(f, f[2:])]
            for k in range(layers):
                dst[(k,) + at] = f[k]


def kernel(
    nz, ny,
    disp, design, void, solid, stiff,
    new_design, sens,
    dpad, fpad, qpad, zbuf, ybuf, void_v, solid_v, energy, amount, low_v, high_v, sens_v, new_v,
    tx, k_high, k_low, cube_yx, weight_yx, inv_weight_yx, z_rows, sums,
    load_sem, store_sem, send1, recv1, send2, recv2, send_r, recv_r,
):
    lz, ly, lx = design.shape
    gz, gy = lax.axis_index("gz"), lax.axis_index("gy")
    has = {
        (1, 0): gz < nz - 1, (-1, 0): gz > 0, (0, 1): gy < ny - 1, (0, -1): gy > 0,
    }
    for dz in (-1, 1):
        for dy in (-1, 1):
            has[dz, dy] = has[dz, 0] & has[0, dy]

    def peer(dz, dy):
        return (lax.rem(gz + dz + nz, nz), lax.rem(gy + dy + ny, ny))

    own_f = fpad.at[H : H + lz, Y0 : Y0 + ly, :]
    loads = [
        pltpu.make_async_copy(disp, dpad.at[:, 0:lz, 0:ly, :], load_sem.at[0]),
        pltpu.make_async_copy(design, own_f, load_sem.at[1]),
        pltpu.make_async_copy(void, void_v, load_sem.at[2]),
        pltpu.make_async_copy(solid, solid_v, load_sem.at[3]),
    ]
    for copy in loads:
        copy.start()

    barrier = pltpu.get_barrier_semaphore()
    partners = [peer(d, 0) for d in range(1, nz)] + [peer(0, d) for d in range(1, ny)]
    partners += [peer(dz, dy) for dz in (-1, 1) for dy in (-1, 1)]
    for partner in partners:
        pl.semaphore_signal(barrier, inc=1, device_id=partner, device_id_type=MESH)

    for pad in (fpad, qpad):
        @pl.when(gz == 0)
        def _():
            pad[0:H] = jnp.zeros_like(pad[0:H])

        @pl.when(gz == nz - 1)
        def _():
            pad[lz + H :] = jnp.zeros_like(pad[lz + H :])

        @pl.when(gy == 0)
        def _():
            pad[:, 0:Y0] = jnp.zeros_like(pad[:, 0:Y0])

        @pl.when(gy == ny - 1)
        def _():
            pad[:, Y0 + ly :] = jnp.zeros_like(pad[:, Y0 + ly :])

    @pl.when(gz == nz - 1)
    def _():
        dpad[:, lz] = jnp.zeros_like(dpad[:, lz])

    @pl.when(gy == ny - 1)
    def _():
        dpad[:, :, ly:] = jnp.zeros_like(dpad[:, :, ly:])

    pl.semaphore_wait(barrier, len(partners))

    near_z = {1: slice(lz - H, lz), -1: slice(0, H), 0: slice(0, lz)}
    near_y = {1: slice(ly - H, ly), -1: slice(0, H), 0: slice(0, ly)}
    far_z = {1: slice(0, H), -1: slice(H + lz, lz + 2 * H), 0: slice(H, H + lz)}
    far_y = {1: slice(Y0 - H, Y0), -1: slice(Y0 + ly, Y0 + ly + H), 0: slice(Y0, Y0 + ly)}
    directions = [(1, 0), (-1, 0), (0, 1), (0, -1), (1, 1), (1, -1), (-1, 1), (-1, -1)]

    def halo(src, src_at, pad, send, recv, n):
        dz, dy = directions[n]
        return pltpu.make_async_remote_copy(
            src_ref=src.at[src_at[0][dz], src_at[1][dy], :],
            dst_ref=pad.at[far_z[dz], far_y[dy], :],
            send_sem=send.at[n], recv_sem=recv.at[n],
            device_id=peer(dz, dy), device_id_type=MESH,
        )

    def start(direction, copy):
        @pl.when(has[direction])
        def _():
            copy.start()

    def wait_recv(direction, copy):
        @pl.when(has[-direction[0], -direction[1]])
        def _():
            copy.wait_recv()

    def wait_send(direction, copy):
        @pl.when(has[direction])
        def _():
            copy.wait_send()

    def nodes(n, direction, layers, rows, to_layers, to_rows):
        return direction, pltpu.make_async_remote_copy(
            src_ref=disp.at[:, layers, rows, :],
            dst_ref=dpad.at[:, to_layers, to_rows, :],
            send_sem=send1.at[8 + n], recv_sem=recv1.at[8 + n],
            device_id=peer(*direction), device_id_type=MESH,
        )

    first_z, top_z = slice(0, 1), slice(lz, lz + 1)
    first_y, top_y = slice(0, 1), slice(ly, ly + 1)
    own_z, own_y = slice(0, lz), slice(0, ly)
    node_copies = [
        nodes(0, (0, -1), own_z, first_y, own_z, top_y),
        nodes(1, (-1, -1), first_z, first_y, top_z, top_y),
        nodes(2, (-1, 0), first_z, own_y, top_z, own_y),
    ]
    design_copies = [
        (directions[n], halo(design, (near_z, near_y), fpad, send1, recv1, n)) for n in range(8)
    ]
    start(*node_copies[0])
    start(*node_copies[1])
    start(*design_copies[0])
    start(*design_copies[1])
    start(*node_copies[2])
    for n in range(2, 8):
        start(*design_copies[n])

    across = jnp.abs(iota((lx, lx), 0) - iota((lx, lx), 1))
    tx[...] = jnp.maximum(4 - across, 0).astype(F32).astype(BF16)
    full_z, full_y = lz * nz, ly * ny
    row_at = iota((ly, lx), 0) + gy * ly
    col_at = iota((ly, lx), 1)
    inv_yx = 1.0 / (line_total(row_at, full_y) * line_total(col_at, lx))
    cube_yx[...] = (-PENALTY) * inv_yx * inv_yx * inv_yx
    spread_yx = line_spread(row_at, full_y) * line_spread(col_at, lx)
    weight_yx[...] = spread_yx
    inv_weight_yx[...] = 1.0 / spread_yx
    layer_at = iota((lz, lx), 0) + gz * lz
    inv_z = 1.0 / line_total(layer_at, full_z)
    spread_z = line_spread(layer_at, full_z)
    z_rows[0] = inv_z * inv_z * inv_z
    z_rows[1] = spread_z
    z_rows[2] = 1.0 / spread_z

    size = 24 * 8
    pick = (lax.shift_right_logical(iota((size, 24), 0), 3) == iota((size, 24), 1)).astype(F32).astype(BF16)
    pick_t = (iota((24, size), 0) == lax.shift_right_logical(iota((24, size), 1), 3)).astype(F32).astype(BF16)
    same = (iota((size, size), 0) & 7) == (iota((size, size), 1) & 7)
    for part, ref in zip(split_bf16(stiff[...]), (k_high, k_low)):
        spread_k = dot(dot(pick, part).astype(BF16), pick_t)
        ref[...] = jnp.where(same, spread_k, 0.0).astype(BF16)

    last_col = iota((8, lx), 1) == lx - 1

    def element_rows(k, tile):
        at = tile * 8
        u = []
        for a in range(2):
            for b in range(2):
                here = [dpad[q, k + a, pl.ds(at + b, 8), :] for q in range(3)]
                u += here
                u += [jnp.where(last_col, 0.0, pltpu.roll(v, lx - 1, 1)) for v in here]
        u = jnp.concatenate(u, axis=0)
        high = u.astype(BF16)
        forces = dot(k_high[...], high) + dot(k_low[...], high)
        terms = (2.0 * u - high.astype(F32)) * forces
        total = jnp.sum(terms.reshape(24, 8, lx), axis=0)
        energy[k, pl.ds(at, 8), :] = jnp.maximum(total, 0.0)

    tiles = ly // 8
    loads[0].wait()

    def inner_layer(k, carry):
        for tile in range(tiles - 1):
            element_rows(k, tile)
        return carry

    lax.fori_loop(0, lz - 1, inner_layer, 0)
    for copy in node_copies:
        wait_recv(*copy)

    def edge_rows(k, carry):
        element_rows(k, tiles - 1)
        return carry

    lax.fori_loop(0, lz - 1, edge_rows, 0)
    for tile in range(tiles):
        element_rows(lz - 1, tile)

    loads[1].wait()
    for copy in design_copies:
        wait_recv(*copy)
    layer_filter(fpad, zbuf, lz)

    def source_layers(first, last):
        for k in range(first, last):
            ybuf[k * ly : (k + 1) * ly, :] = row_filter(zbuf, k, ly)
        high, low = split_bf16(ybuf[first * ly : last * ly, :])
        filtered = dot(high, tx[...]) + dot(low, tx[...])
        for k in range(first, last):
            f = filtered[(k - first) * ly : (k - first + 1) * ly]
            ybuf[k * ly : (k + 1) * ly, :] = (
                f * f * energy[k] * (cube_yx[...] * z_rows[0, k : k + 1, :])
            )
        high, low = split_bf16(ybuf[first * ly : last * ly, :])
        filtered = dot(high, tx[...]) + dot(low, tx[...])
        for k in range(first, last):
            qpad[H + k, Y0 : Y0 + ly, :] = filtered[(k - first) * ly : (k - first + 1) * ly]

    own_zq = {1: slice(lz, lz + H), -1: slice(H, 2 * H), 0: slice(H, H + lz)}
    own_yq = {1: slice(Y0 + ly - H, Y0 + ly), -1: slice(Y0, Y0 + H), 0: slice(Y0, Y0 + ly)}
    source_copies = [
        (directions[n], halo(qpad, (own_zq, own_yq), qpad, send2, recv2, n)) for n in range(8)
    ]
    source_layers(lz - H, lz)
    start(*source_copies[0])
    source_layers(0, H)
    start(*source_copies[1])
    for n in range(4, 8):
        start(*source_copies[n])
    source_layers(H, lz // 2)
    source_layers(lz // 2, lz - H)
    start(*source_copies[2])
    start(*source_copies[3])

    loads[2].wait()
    loads[3].wait()

    def bounds(k, carry):
        weight = weight_yx[...] * z_rows[1, pl.ds(k, 1), :]
        d = fpad[H + k, Y0 : Y0 + ly, :]
        is_solid, is_void = solid_v[k] == 1, void_v[k] == 1
        low = jnp.maximum(d - MOVE_LIMIT, 0.0) * weight
        high = jnp.minimum(d + MOVE_LIMIT, 1.0) * weight
        low_v[k] = jnp.where(is_solid, weight, jnp.where(is_void, 0.0, low))
        high_v[k] = jnp.where(is_solid, weight, jnp.where(is_void, 0.0, high))
        return carry

    lax.fori_loop(0, lz, bounds, 0)

    for copy in source_copies:
        wait_recv(*copy)
    layer_filter(qpad, zbuf, lz)
    for k in range(lz):
        s = row_filter(zbuf, k, ly)
        sens_v[k] = s
        d = fpad[H + k, Y0 : Y0 + ly, :]
        amount[k] = d * jnp.sqrt(-s * (weight_yx[...] * z_rows[1, k : k + 1, :]))
    store_sens = pltpu.make_async_copy(sens_v, sens, store_sem.at[0])
    store_sens.start()

    lane = iota((1, 128), 1)
    points = SPLIT + 1
    rows_p = -(-points // 8) * 8

    def exchange(row, n, axis_at, size, to):
        slot = pl.ds(axis_at, 1)
        sums[n, slot, :] = row
        copies = []
        for d in range(1, size):
            copies.append(
                pltpu.make_async_remote_copy(
                    src_ref=sums.at[n, slot, :], dst_ref=sums.at[n, slot, :],
                    send_sem=send_r.at[n], recv_sem=recv_r.at[n],
                    device_id=to(d), device_id_type=MESH,
                )
            )
        for copy in copies:
            copy.start()
        everyone = sums.at[n, pl.ds(0, size - 1), :]
        pltpu.make_async_copy(everyone, everyone, recv_r.at[n]).wait()
        total = jnp.sum(sums[n, 0:size, :], axis=0, keepdims=True)
        return total

    def volumes(scale, step, first):
        factors = [first * 2.718281828459045 ** (-0.5 * step * j) for j in range(points)]

        def layer(k, totals):
            totals = list(totals)
            for r in range(0, ly, 8):
                for c in range(0, lx, 128):
                    at = (k, slice(r, r + 8), slice(c, c + 128))
                    a, low, high = amount[at], low_v[at], high_v[at]
                    if scale is not None:
                        a = a * scale
                    for j in range(points):
                        totals[j] = totals[j] + jnp.minimum(jnp.maximum(a * factors[j], low), high)
            return tuple(totals)

        totals = lax.fori_loop(
            0, lz, layer, tuple(jnp.zeros((8, 128), F32) for _ in range(points))
        )
        sub = iota((rows_p, 128), 0)
        stacked = jnp.zeros((rows_p, 128), F32)
        for j in range(points):
            stacked = jnp.where(sub == j, jnp.sum(totals[j], axis=0, keepdims=True), stacked)
        line = jnp.sum(stacked, axis=1, keepdims=True)
        return jnp.sum(jnp.where(sub == iota((rows_p, 128), 1), line, 0.0), axis=0, keepdims=True)

    def everywhere(row, n):
        row = exchange(row, 2 * n, gz, nz, lambda d: peer(d, 0))
        return exchange(row, 2 * n + 1, gy, ny, lambda d: peer(0, d))

    target = VOLUME_FRACTION * full_z * full_y * lx
    inside = (lane >= 1) & (lane < SPLIT)

    def cell(row):
        above = jnp.where(inside & (row > target), 1.0, 0.0)
        return jnp.sum(above, axis=1, keepdims=True)

    wide = (HIGH_LOG - LOW_LOG) / SPLIT
    fine = wide / SPLIT
    row = everywhere(volumes(None, wide, 2.718281828459045 ** (-0.5 * LOW_LOG)), 0)
    low = LOW_LOG + wide * cell(row)
    row = everywhere(volumes(jnp.exp(-0.5 * low), fine, 1.0), 1)
    index = cell(row)
    at_lane = lane.astype(F32)
    low_volume = jnp.sum(jnp.where(at_lane == index, row, 0.0), axis=1, keepdims=True)
    high_volume = jnp.sum(jnp.where(at_lane == index + 1.0, row, 0.0), axis=1, keepdims=True)
    low = low + fine * index
    final = low + fine * ((low_volume - target) / (low_volume - high_volume))
    factor = jnp.exp(-0.5 * final)

    def finish(k, carry):
        d = fpad[H + k, Y0 : Y0 + ly, :]
        moved = amount[k] * (inv_weight_yx[...] * (z_rows[2, pl.ds(k, 1), :] * factor))
        moved = jnp.minimum(
            jnp.maximum(moved, jnp.maximum(d - MOVE_LIMIT, 0.0)), jnp.minimum(d + MOVE_LIMIT, 1.0)
        )
        new_v[k] = jnp.where(solid_v[k] == 1, 1.0, jnp.where(void_v[k] == 1, 0.0, moved))
        return carry

    lax.fori_loop(0, lz, finish, 0)
    store_new = pltpu.make_async_copy(new_v, new_design, store_sem.at[1])
    store_new.start()

    for copy in node_copies + design_copies + source_copies:
        wait_send(*copy)
    for n, size in enumerate((nz, ny, nz, ny)):
        everyone = sums.at[n, pl.ds(0, size - 1), :]
        pltpu.make_async_copy(everyone, everyone, send_r.at[n]).wait()
    store_sens.wait()
    store_new.wait()


def per_device(displacement, design, void_mask, solid_mask, stiffness):
    nz, ny = lax.axis_size("gz"), lax.axis_size("gy")
    lz, ly, lx = design.shape
    brick = jax.ShapeDtypeStruct(design.shape, F32)
    padded = (lz + 2 * H, ly + 16, lx)
    anywhere = pl.BlockSpec(memory_space=pl.ANY)
    new_design, sens = pl.pallas_call(
        functools.partial(kernel, nz, ny),
        out_shape=(brick, brick),
        in_specs=[anywhere] * 4 + [pl.BlockSpec(memory_space=pltpu.VMEM)],
        out_specs=(anywhere, anywhere),
        scratch_shapes=[
            pltpu.VMEM((3, lz + 1, ly + 8, lx), F32),
            pltpu.VMEM(padded, F32),
            pltpu.VMEM(padded, F32),
            pltpu.VMEM((lz, ly + 16, lx), F32),
            pltpu.VMEM((lz * ly, lx), F32),
            pltpu.VMEM(design.shape, jnp.int32),
            pltpu.VMEM(design.shape, jnp.int32),
            pltpu.VMEM(design.shape, F32),
            pltpu.VMEM(design.shape, F32),
            pltpu.VMEM(design.shape, F32),
            pltpu.VMEM(design.shape, F32),
            pltpu.VMEM(design.shape, F32),
            pltpu.VMEM(design.shape, F32),
            pltpu.VMEM((lx, lx), BF16),
            pltpu.VMEM((192, 192), BF16),
            pltpu.VMEM((192, 192), BF16),
            pltpu.VMEM((ly, lx), F32),
            pltpu.VMEM((ly, lx), F32),
            pltpu.VMEM((ly, lx), F32),
            pltpu.VMEM((3, lz, lx), F32),
            pltpu.VMEM((4, max(nz, ny), 128), F32),
            pltpu.SemaphoreType.DMA((4,)),
            pltpu.SemaphoreType.DMA((2,)),
            pltpu.SemaphoreType.DMA((11,)),
            pltpu.SemaphoreType.DMA((11,)),
            pltpu.SemaphoreType.DMA((8,)),
            pltpu.SemaphoreType.DMA((8,)),
            pltpu.SemaphoreType.DMA((4,)),
            pltpu.SemaphoreType.DMA((4,)),
        ],
        compiler_params=pltpu.CompilerParams(
            collective_id=0, has_side_effects=True, vmem_limit_bytes=40 * 1024 * 1024
        ),
    )(displacement, design, void_mask, solid_mask, stiffness)
    return new_design, sens


def solution(mesh):
    return jax.shard_map(
        per_device,
        mesh=mesh,
        in_specs=(
            P(None, "gz", "gy", None),
            P("gz", "gy", None),
            P("gz", "gy", None),
            P("gz", "gy", None),
            P(),
        ),
        out_specs=(P("gz", "gy", None), P("gz", "gy", None)),
        check_vma=False,
    )
```

time: 1090 us -> 63.5 us (0.06)
  blocking collectives: 676 us -> 0 us
  starting transfers between devices: 112 us -> 0 us
  local copies, waits for them, and re-layouts: 116 us -> 6.82 us
  waiting for transfers between devices: 78 us -> 0 us
  Pallas kernels: 0 us -> 55.7 us
  other arithmetic: 35.2 us -> 0 us
  loops' own time: 33.5 us -> 0 us
  between operations: 18.7 us -> 0.65 us
  matrix products: 13.2 us -> 0 us
    psum x8 -> x0, blocking collectives: 676 us -> none  [volumes(): return lax.psum(local_sums, ('gz', 'gy'))]
    ppermute x46 -> x0, starting transfers between devices: 112 us -> none  [the longest x22 70.7 us: padded_2(): lax.ppermute(lax.slice_in_dim(block, block.shape[dim] - width, None, axis...]
    ppermute x46 -> x0, waiting for transfers between devices: 78 us -> none  [the longest x22 67.9 us: padded_2(): lax.ppermute(lax.slice_in_dim(block, 0, width, axis=dim), axis, backward)]
    squeeze x16 -> x0, local copies, waits for them, and re-layouts: 69.8 us -> none  [one_layer(): stacked = jnp.stack(corners)]
    pallas_call x0 -> x1, Pallas kernels: none -> 55.7 us  [per_device(): pl.pallas_call(functools.partial(kernel, nz, ny), out_shape=(brick, brick...]
    another operation x1 -> x0, loops' own time: 33.5 us -> none  [energies(): return lax.map(one_layer, jnp.arange(layer_count, dtype=jnp.int32))]
    another operation x16 -> x0, local copies, waits for them, and re-layouts: 18.5 us -> none  [one_layer(): stacked = jnp.stack(corners)]
    reduce_sum x15 -> x0, other arithmetic: 15.2 us -> none  [the longest x9 14.4 us: volumes(): local_sums = jnp.sum(filtered * inverse_total[None], axis=(1, 2, 3))]
  transfers between devices with their start and end apart: 46 -> 0, of which waited for: 29 -> 0; matrix products, arithmetic and copies ran while one was open for 12% -> 0% of each run, Pallas kernels for 0% -> 0%
where the time goes in v1:
time: 63.5 us; the launch traced here: 63.2 us
  Pallas kernels  55.7 us (88%)
  local copies, waits for them, and re-layouts  6.82 us (11%)
  between operations  0.65 us (1%)
    pallas_call x1, Pallas kernels, per_device(): pl.pallas_call(functools.partial(kernel, nz, ny), out_shape=(brick, brick...  55.7 us
    unnamed x12, local copies, waits for them, and re-layouts  6.82 us

profile of v1, /device:TPU:1, one launch (start us, length us, event | category | flops | bytes accessed | tf_op | source)
XLA Modules:
  0.0 63.2 jit_solution(2531297629803738301)
XLA Ops:
  0.6 0.0 copy-start
  0.6 1.4 %copy-done = f32[3,16,32,256]{3,2,1,0:T(8,128)S(1)} copy-done((f32[3,16,32,256]{3,2,1,0:T(8,128)S(1)}, f32[3,16,32,256]{3,2,1,0:T(8,128)}, u32[]{:S(2)}) %copy-start) | copy-done | bytes 1572888
  2.0 0.0 copy-start.1
  2.0 1.0 %copy-done.1 = f32[16,32,256]{2,1,0:T(8,128)S(1)} copy-done((f32[16,32,256]{2,1,0:T(8,128)S(1)}, f32[16,32,256]{2,1,0:T(8,128)}, u32[]{:S(2)}) %copy-start.1) | copy-done | bytes 524312
  3.1 0.0 copy-start.2
  3.1 1.0 %copy-done.2 = s32[16,32,256]{2,1,0:T(8,128)S(1)} copy-done((s32[16,32,256]{2,1,0:T(8,128)S(1)}, s32[16,32,256]{2,1,0:T(8,128)}, u32[]{:S(2)}) %copy-start.2) | copy-done | bytes 524312
  4.1 0.0 copy-start.3
  4.1 1.0 %copy-done.3 = s32[16,32,256]{2,1,0:T(8,128)S(1)} copy-done((s32[16,32,256]{2,1,0:T(8,128)S(1)}, s32[16,32,256]{2,1,0:T(8,128)}, u32[]{:S(2)}) %copy-start.3) | copy-done | bytes 524312
  5.2 0.0 copy-start.4
  5.2 0.7 %copy-done.4 = f32[24,24]{1,0:T(8,128)S(1)} copy-done((f32[24,24]{1,0:T(8,128)S(1)}, f32[24,24]{1,0:T(8,128)}, u32[]{:S(2)}) %copy-start.4) | copy-done | bytes 2328
  5.9 55.7 %shard_map.68 = (f32[16,32,256]{2,1,0:T(8,128)S(1)}, f32[16,32,256]{2,1,0:T(8,128)S(1)}) custom-call(f32[3,16,32,256]{3,2,1,0:T(8,128)S(1)} %copy-done, f32[16,32,256]{2,1,0:T(8,128)S(1)} %copy-done.1, s32[16,32,256]{2,1,0:T(8,128)S(1)} %copy-done.2, s32[16,32,256]{2,1,0:T(8,128)S(1)} %copy-done.3, f32[24,24]{1,0:T(8,128)S(1)} %copy-done.4), custom_call_target="tpu_custom_call" | custom-call | tf_op jit(solution)/shard_map/pallas_call | solution.py:421
  61.6 0.8 %copy.9 = f32[16,32,256]{2,1,0:T(8,128)} copy(f32[16,32,256]{2,1,0:T(8,128)S(1)} %get-tuple-element.4) | data formatting | bytes 1048576
  62.4 0.8 %copy.10 = f32[16,32,256]{2,1,0:T(8,128)} copy(f32[16,32,256]{2,1,0:T(8,128)S(1)} %get-tuple-element.5) | data formatting | bytes 1048576
Async XLA Ops:
  0.6 1.4 %copy-start = (f32[3,16,32,256]{3,2,1,0:T(8,128)S(1)}, f32[3,16,32,256]{3,2,1,0:T(8,128)}, u32[]{:S(2)}) copy-start(f32[3,16,32,256]{3,2,1,0:T(8,128)} %disp.1) | copy-start | bytes 4718596
  2.0 1.0 %copy-start.1 = (f32[16,32,256]{2,1,0:T(8,128)S(1)}, f32[16,32,256]{2,1,0:T(8,128)}, u32[]{:S(2)}) copy-start(f32[16,32,256]{2,1,0:T(8,128)} %design.1) | copy-start | bytes 1572868
  3.1 1.0 %copy-start.2 = (s32[16,32,256]{2,1,0:T(8,128)S(1)}, s32[16,32,256]{2,1,0:T(8,128)}, u32[]{:S(2)}) copy-start(s32[16,32,256]{2,1,0:T(8,128)} %void.1) | copy-start | bytes 1572868
  4.1 1.0 %copy-start.3 = (s32[16,32,256]{2,1,0:T(8,128)S(1)}, s32[16,32,256]{2,1,0:T(8,128)}, u32[]{:S(2)}) copy-start(s32[16,32,256]{2,1,0:T(8,128)} %solid.1) | copy-start | bytes 1572868
  5.2 0.7 %copy-start.4 = (f32[24,24]{1,0:T(8,128)S(1)}, f32[24,24]{1,0:T(8,128)}, u32[]{:S(2)}) copy-start(f32[24,24]{1,0:T(8,128)} %stiff.1) | copy-start | bytes 6916

commit v2 on v1

--- a/solution.py
+++ b/solution.py
@@ -55,8 +55,9 @@
     return jnp.dot(a, b, preferred_element_type=F32)
 
 
-def row_filter(ref, layer, rows):
-    c = [ref[layer, Y0 - H + t : Y0 - H + t + rows, :] for t in range(7)]
+def row_filter(ref, layer, rows, first=0):
+    at = Y0 - H + first
+    c = [ref[layer, at + t : at + t + rows, :] for t in range(7)]
     return (c[0] + c[6]) + 2.0 * (c[1] + c[5]) + 3.0 * (c[2] + c[4]) + 4.0 * c[3]
 
 
@@ -78,9 +79,9 @@
     nz, ny,
     disp, design, void, solid, stiff,
     new_design, sens,
-    dpad, fpad, qpad, zbuf, ybuf, void_v, solid_v, energy, amount, low_v, high_v, sens_v, new_v,
+    dpad, fpad, qpad, zbuf, void_v, solid_v, energy, amount, low_v, high_v, sens_v, new_v,
     tx, k_high, k_low, cube_yx, weight_yx, inv_weight_yx, z_rows, sums,
-    load_sem, store_sem, send1, recv1, send2, recv2, send_r, recv_r,
+    load_sem, store_sem, send1, recv1, send2, recv2, send_r, recv_r, known,
 ):
     lz, ly, lx = design.shape
     gz, gy = lax.axis_index("gz"), lax.axis_index("gy")
@@ -105,11 +106,24 @@
         copy.start()
 
     barrier = pltpu.get_barrier_semaphore()
-    partners = [peer(d, 0) for d in range(1, nz)] + [peer(0, d) for d in range(1, ny)]
+    partners = [peer(1, 0), peer(-1, 0), peer(0, 1), peer(0, -1)]
     partners += [peer(dz, dy) for dz in (-1, 1) for dy in (-1, 1)]
     for partner in partners:
         pl.semaphore_signal(barrier, inc=1, device_id=partner, device_id_type=MESH)
 
+    def tell(level):
+        reach = 1 << level
+        for axis, way in enumerate(((reach, 0), (0, reach))):
+            for sign in (1, -1):
+                pl.semaphore_signal(
+                    known.at[2 * level + axis], inc=1,
+                    device_id=peer(sign * way[0], sign * way[1]), device_id_type=MESH,
+                )
+
+    def hear(level):
+        for axis in range(2):
+            pl.semaphore_wait(known.at[2 * level + axis], 2)
+
     for pad in (fpad, qpad):
         @pl.when(gz == 0)
         def _():
@@ -136,6 +150,7 @@
         dpad[:, :, ly:] = jnp.zeros_like(dpad[:, :, ly:])
 
     pl.semaphore_wait(barrier, len(partners))
+    tell(0)
 
     near_z = {1: slice(lz - H, lz), -1: slice(0, H), 0: slice(0, lz)}
     near_y = {1: slice(ly - H, ly), -1: slice(0, H), 0: slice(0, ly)}
@@ -186,11 +201,10 @@
     design_copies = [
         (directions[n], halo(design, (near_z, near_y), fpad, send1, recv1, n)) for n in range(8)
     ]
+    start(*design_copies[0])
+    start(*design_copies[1])
     start(*node_copies[0])
     start(*node_copies[1])
-    start(*design_copies[0])
-    start(*design_copies[1])
-    start(*node_copies[2])
     for n in range(2, 8):
         start(*design_copies[n])
 
@@ -237,60 +251,77 @@
         energy[k, pl.ds(at, 8), :] = jnp.maximum(total, 0.0)
 
     tiles = ly // 8
+
+    def energy_of(count, layer_of, tiles_of):
+        def body(n, carry):
+            for k in layer_of(n):
+                for tile in tiles_of:
+                    element_rows(k, tile)
+            return carry
+
+        lax.fori_loop(0, count, body, 0)
+
     loads[0].wait()
-
-    def inner_layer(k, carry):
-        for tile in range(tiles - 1):
-            element_rows(k, tile)
-        return carry
-
-    lax.fori_loop(0, lz - 1, inner_layer, 0)
-    for copy in node_copies:
-        wait_recv(*copy)
-
-    def edge_rows(k, carry):
-        element_rows(k, tiles - 1)
-        return carry
-
-    lax.fori_loop(0, lz - 1, edge_rows, 0)
-    for tile in range(tiles):
-        element_rows(lz - 1, tile)
+    inner = lz - 2 * H
+    energy_of(2 * H - 1, lambda n: [n + (n // H) * inner], range(tiles - 1))
+    start(*node_copies[2])
+    hear(0)
+    tell(1)
+    energy_of(inner // 2, lambda n: [H + 2 * n, H + 2 * n + 1], [0])
+    wait_recv(*node_copies[0])
+    wait_recv(*node_copies[1])
+    energy_of((lz - 1) // 3, lambda n: [3 * n, 3 * n + 1, 3 * n + 2], [tiles - 1])
 
     loads[1].wait()
     for copy in design_copies:
         wait_recv(*copy)
     layer_filter(fpad, zbuf, lz)
 
-    def source_layers(first, last):
-        for k in range(first, last):
-            ybuf[k * ly : (k + 1) * ly, :] = row_filter(zbuf, k, ly)
-        high, low = split_bf16(ybuf[first * ly : last * ly, :])
-        filtered = dot(high, tx[...]) + dot(low, tx[...])
-        for k in range(first, last):
-            f = filtered[(k - first) * ly : (k - first + 1) * ly]
-            ybuf[k * ly : (k + 1) * ly, :] = (
-                f * f * energy[k] * (cube_yx[...] * z_rows[0, k : k + 1, :])
-            )
-        high, low = split_bf16(ybuf[first * ly : last * ly, :])
-        filtered = dot(high, tx[...]) + dot(low, tx[...])
-        for k in range(first, last):
-            qpad[H + k, Y0 : Y0 + ly, :] = filtered[(k - first) * ly : (k - first + 1) * ly]
+    def source(layers, first, last):
+        n = last - first
+        f = jnp.concatenate([row_filter(zbuf, k, n, first) for k in layers], axis=0)
+        high, low = split_bf16(f)
+        f = dot(high, tx[...]) + dot(low, tx[...])
+        cube = cube_yx[first:last]
+        f = jnp.concatenate(
+            [
+                f[i * n : (i + 1) * n] * f[i * n : (i + 1) * n]
+                * (energy[k, first:last] * (cube * z_rows[0, k : k + 1, :]))
+                for i, k in enumerate(layers)
+            ],
+            axis=0,
+        )
+        high, low = split_bf16(f)
+        f = dot(high, tx[...]) + dot(low, tx[...])
+        for i, k in enumerate(layers):
+            qpad[H + k, Y0 + first : Y0 + last, :] = f[i * n : (i + 1) * n]
 
     own_zq = {1: slice(lz, lz + H), -1: slice(H, 2 * H), 0: slice(H, H + lz)}
     own_yq = {1: slice(Y0 + ly - H, Y0 + ly), -1: slice(Y0, Y0 + H), 0: slice(Y0, Y0 + ly)}
     source_copies = [
         (directions[n], halo(qpad, (own_zq, own_yq), qpad, send2, recv2, n)) for n in range(8)
     ]
-    source_layers(lz - H, lz)
+    source(range(H), 0, ly)
+    start(*source_copies[1])
+    start(*source_copies[6])
+    start(*source_copies[7])
+    wait_recv(*node_copies[2])
+    for tile in range(tiles):
+        element_rows(lz - 1, tile)
+    source(range(lz - H, lz), 0, ly)
     start(*source_copies[0])
-    source_layers(0, H)
-    start(*source_copies[1])
-    for n in range(4, 8):
-        start(*source_copies[n])
-    source_layers(H, lz // 2)
-    source_layers(lz // 2, lz - H)
+    start(*source_copies[4])
+    start(*source_copies[5])
+    middle = range(H, lz - H)
+    source(middle, 0, 8)
+    start(*source_copies[3])
+    source(middle, ly - 8, ly)
     start(*source_copies[2])
-    start(*source_copies[3])
+    hear(1)
+    tell(2)
+    energy_of(inner // 2, lambda n: [H + 2 * n, H + 2 * n + 1], range(1, tiles - 1))
+    source(range(H, lz // 2), 8, ly - 8)
+    source(range(lz // 2, lz - H), 8, ly - 8)
 
     loads[2].wait()
     loads[3].wait()
@@ -323,26 +354,25 @@
     rows_p = -(-points // 8) * 8
 
     def exchange(row, n, axis_at, size, to):
-        slot = pl.ds(axis_at, 1)
-        sums[n, slot, :] = row
+        sums[n, axis_at] = row
         copies = []
         for d in range(1, size):
             copies.append(
                 pltpu.make_async_remote_copy(
-                    src_ref=sums.at[n, slot, :], dst_ref=sums.at[n, slot, :],
+                    src_ref=sums.at[n, axis_at], dst_ref=sums.at[n, axis_at],
                     send_sem=send_r.at[n], recv_sem=recv_r.at[n],
                     device_id=to(d), device_id_type=MESH,
                 )
             )
         for copy in copies:
             copy.start()
-        everyone = sums.at[n, pl.ds(0, size - 1), :]
+        everyone = sums.at[n, 0 : size - 1]
         pltpu.make_async_copy(everyone, everyone, recv_r.at[n]).wait()
-        total = jnp.sum(sums[n, 0:size, :], axis=0, keepdims=True)
-        return total
-
-    def volumes(scale, step, first):
-        factors = [first * 2.718281828459045 ** (-0.5 * step * j) for j in range(points)]
+        return jnp.sum(sums[n, 0:size], axis=0)
+
+    def volumes(scale, step, first, at_lanes):
+        factors = [first * 2.718281828459045 ** (-0.5 * step * j) for j in at_lanes]
+        points = len(factors)
 
         def layer(k, totals):
             totals = list(totals)
@@ -362,7 +392,7 @@
         sub = iota((rows_p, 128), 0)
         stacked = jnp.zeros((rows_p, 128), F32)
         for j in range(points):
-            stacked = jnp.where(sub == j, jnp.sum(totals[j], axis=0, keepdims=True), stacked)
+            stacked = jnp.where(sub == at_lanes[j], jnp.sum(totals[j], axis=0, keepdims=True), stacked)
         line = jnp.sum(stacked, axis=1, keepdims=True)
         return jnp.sum(jnp.where(sub == iota((rows_p, 128), 1), line, 0.0), axis=0, keepdims=True)
 
@@ -379,13 +409,21 @@
 
     wide = (HIGH_LOG - LOW_LOG) / SPLIT
     fine = wide / SPLIT
-    row = everywhere(volumes(None, wide, 2.718281828459045 ** (-0.5 * LOW_LOG)), 0)
-    low = LOW_LOG + wide * cell(row)
-    row = everywhere(volumes(jnp.exp(-0.5 * low), fine, 1.0), 1)
+    at_lane = lane.astype(F32)
+
+    def entry(row, index):
+        return jnp.sum(jnp.where(at_lane == index, row, 0.0), axis=1, keepdims=True)
+
+    start_factor = 2.718281828459045 ** (-0.5 * LOW_LOG)
+    hear(2)
+    row = everywhere(volumes(None, wide, start_factor, range(points)), 0)
     index = cell(row)
-    at_lane = lane.astype(F32)
-    low_volume = jnp.sum(jnp.where(at_lane == index, row, 0.0), axis=1, keepdims=True)
-    high_volume = jnp.sum(jnp.where(at_lane == index + 1.0, row, 0.0), axis=1, keepdims=True)
+    low = LOW_LOG + wide * index
+    ends = (entry(row, index), entry(row, index + 1.0))
+    row = everywhere(volumes(jnp.exp(-0.5 * low), fine, 1.0, range(1, SPLIT)), 1)
+    row = jnp.where(lane == 0, ends[0], jnp.where(lane == SPLIT, ends[1], row))
+    index = cell(row)
+    low_volume, high_volume = entry(row, index), entry(row, index + 1.0)
     low = low + fine * index
     final = low + fine * ((low_volume - target) / (low_volume - high_volume))
     factor = jnp.exp(-0.5 * final)
@@ -406,7 +444,7 @@
     for copy in node_copies + design_copies + source_copies:
         wait_send(*copy)
     for n, size in enumerate((nz, ny, nz, ny)):
-        everyone = sums.at[n, pl.ds(0, size - 1), :]
+        everyone = sums.at[n, 0 : size - 1]
         pltpu.make_async_copy(everyone, everyone, send_r.at[n]).wait()
     store_sens.wait()
     store_new.wait()
@@ -417,7 +455,7 @@
     lz, ly, lx = design.shape
     brick = jax.ShapeDtypeStruct(design.shape, F32)
     padded = (lz + 2 * H, ly + 16, lx)
-    anywhere = pl.BlockSpec(memory_space=pl.ANY)
+    anywhere = pl.BlockSpec(memory_space=pltpu.HBM)
     new_design, sens = pl.pallas_call(
         functools.partial(kernel, nz, ny),
         out_shape=(brick, brick),
@@ -428,7 +466,6 @@
             pltpu.VMEM(padded, F32),
             pltpu.VMEM(padded, F32),
             pltpu.VMEM((lz, ly + 16, lx), F32),
-            pltpu.VMEM((lz * ly, lx), F32),
             pltpu.VMEM(design.shape, jnp.int32),
             pltpu.VMEM(design.shape, jnp.int32),
             pltpu.VMEM(design.shape, F32),
@@ -444,7 +481,7 @@
             pltpu.VMEM((ly, lx), F32),
             pltpu.VMEM((ly, lx), F32),
             pltpu.VMEM((3, lz, lx), F32),
-            pltpu.VMEM((4, max(nz, ny), 128), F32),
+            pltpu.VMEM((4, max(nz, ny), 1, 128), F32),
             pltpu.SemaphoreType.DMA((4,)),
             pltpu.SemaphoreType.DMA((2,)),
             pltpu.SemaphoreType.DMA((11,)),
@@ -453,9 +490,10 @@
             pltpu.SemaphoreType.DMA((8,)),
             pltpu.SemaphoreType.DMA((4,)),
             pltpu.SemaphoreType.DMA((4,)),
+            pltpu.SemaphoreType.REGULAR((6,)),
         ],
         compiler_params=pltpu.CompilerParams(
-            collective_id=0, has_side_effects=True, vmem_limit_bytes=40 * 1024 * 1024
+            collective_id=0, has_side_effects=True, vmem_limit_bytes=60 * 1024 * 1024
         ),
     )(displacement, design, void_mask, solid_mask, stiffness)
     return new_design, sens

time: 63.5 us -> 56.4 us (0.89)
  Pallas kernels: 55.7 us -> 51.8 us
  local copies, waits for them, and re-layouts: 6.82 us -> 3.76 us
    pallas_call x1, Pallas kernels: 55.7 us -> 51.8 us  [per_device(): pl.pallas_call(functools.partial(kernel, nz, ny), out_shape=(brick, brick...]
    unnamed x12 -> x2, local copies, waits for them, and re-layouts: 6.82 us -> 3.76 us
where the time goes in v2:
time: 56.4 us; the launch traced here: 56.2 us
  Pallas kernels  51.8 us (92%)
  local copies, waits for them, and re-layouts  3.76 us (7%)
  between operations  0.64 us (1%)
    pallas_call x1, Pallas kernels, per_device(): pl.pallas_call(functools.partial(kernel, nz, ny), out_shape=(brick, brick...  51.8 us
    unnamed x2, local copies, waits for them, and re-layouts  3.76 us

profile of v2, /device:TPU:1, one launch (start us, length us, event | category | flops | bytes accessed | tf_op | source)
XLA Modules:
  0.0 56.2 jit_solution(324357972475097039)
XLA Ops:
  0.6 51.8 %shard_map.68 = (f32[16,32,256]{2,1,0:T(8,128)}, f32[16,32,256]{2,1,0:T(8,128)}) custom-call(f32[3,16,32,256]{3,2,1,0:T(8,128)} %disp.1, f32[16,32,256]{2,1,0:T(8,128)} %design.1, s32[16,32,256]{2,1,0:T(8,128)} %void.1, s32[16,32,256]{2,1,0:T(8,128)} %solid.1, f32[24,24]{1,0:T(8,128)} %stiff.1), custom_call_target="tpu_custom_call" | custom-call | tf_op jit(solution)/shard_map/pallas_call | solution.py:459
  52.4 1.9 %copy.9 = f32[16,32,256]{2,1,0:T(8,128)} copy(f32[16,32,256]{2,1,0:T(8,128)} %get-tuple-element.4) | data formatting | bytes 1048576
  54.3 1.9 %copy.10 = f32[16,32,256]{2,1,0:T(8,128)} copy(f32[16,32,256]{2,1,0:T(8,128)} %get-tuple-element.5) | data formatting | bytes 1048576

commit v3 on v2

v3 whole, which is shorter than its diff:
```python
import functools

import jax
import jax.numpy as jnp
from jax import lax
from jax.experimental import pallas as pl
from jax.experimental.pallas import tpu as pltpu
from jax.sharding import PartitionSpec as P

MESH = pl.DeviceIdType.MESH
NEAR_Z = [(d, 0) for d in (2, -2, 3, -3, 4, -4, 5, -5, 6, -6)]
NEAR_Y = [(0, d) for d in (2, -2, 8, 7, 9, 6, 10)]
F32 = jnp.float32
BF16 = jnp.bfloat16

TAPS = (1.0, 2.0, 3.0, 4.0, 3.0, 2.0, 1.0)
LOW_LOG = -25.0
HIGH_LOG = 25.0
MOVE_LIMIT = 0.2
VOLUME_FRACTION = 0.5
PENALTY = 3.0
SPLIT = 16
GRID = SPLIT * SPLIT
FINE = (HIGH_LOG - LOW_LOG) / GRID
ROUGH = 64
WINDOW = 14
E = 2.718281828459045

H = 3
Y0 = 8


def line_total(p, extent):
    low = jnp.maximum(3 - p, 0)
    high = jnp.maximum(p - (extent - 4), 0)
    missing = low * (low + 1) + high * (high + 1)
    return 16.0 - 0.5 * missing.astype(F32)


def line_spread(p, extent):
    total = None
    for d in range(-3, 4):
        near = p + d
        term = jnp.where(
            (near >= 0) & (near < extent), TAPS[d + 3] / line_total(near, extent), 0.0
        )
        total = term if total is None else total + term
    return total


def iota(shape, dim):
    return lax.broadcasted_iota(jnp.int32, shape, dim)


def split_bf16(x):
    high = x.astype(BF16)
    low = (x - high.astype(F32)).astype(BF16)
    return high, low


def dot(a, b):
    return jnp.dot(a, b, preferred_element_type=F32)


def row_filter(ref, layer, rows, first=0):
    at = Y0 - H + first
    c = [ref[layer, at + t : at + t + rows, :] for t in range(7)]
    return (c[0] + c[6]) + 2.0 * (c[1] + c[5]) + 3.0 * (c[2] + c[4]) + 4.0 * c[3]


def layer_filter(src, dst, layers, first=0, rows=None, first_row=0):
    rows = src.shape[1] if rows is None else rows
    for r in range(0, rows, 8):
        for c in range(0, src.shape[2], 128):
            col = slice(c, c + 128)
            f = [src[first + k, first_row + r : first_row + r + 8, col] for k in range(layers + 2 * H)]
            f = [a + b for a, b in zip(f, f[1:])]
            f = [a + b for a, b in zip(f, f[2:])]
            f = [a + b for a, b in zip(f, f[1:])]
            f = [a + b for a, b in zip(f, f[2:])]
            for k in range(layers):
                dst[k, r : r + 8, col] = f[k]


def sum_start(n, row, at, size, to, sums, send, recv):
    sums[n, at] = row
    copies = [
        pltpu.make_async_remote_copy(
            src_ref=sums.at[n, at], dst_ref=sums.at[n, at],
            send_sem=send.at[n], recv_sem=recv.at[n],
            device_id=to(d), device_id_type=MESH,
        )
        for d in range(1, size)
    ]
    for copy in copies:
        copy.start()


def sum_finish(n, size, sums, recv):
    everyone = sums.at[n, 0 : size - 1]
    pltpu.make_async_copy(everyone, everyone, recv.at[n]).wait()
    return jnp.sum(sums[n, 0:size], axis=0)


def sum_sent(n, size, sums, send):
    everyone = sums.at[n, 0 : size - 1]
    pltpu.make_async_copy(everyone, everyone, send.at[n]).wait()


def to_lanes(rows, lanes):
    count = -(-(max(lanes) + 1) // 8) * 8
    sub = iota((count, 128), 0)
    stacked = jnp.zeros((count, 128), F32)
    for row, j in zip(rows, lanes):
        stacked = jnp.where(sub == j, jnp.sum(row, axis=0, keepdims=True), stacked)
    line = jnp.sum(stacked, axis=1, keepdims=True)
    return jnp.sum(jnp.where(sub == iota((count, 128), 1), line, 0.0), axis=0, keepdims=True)


def volumes(amount, low_v, high_v, scale, factors, lanes):
    lz, ly, lx = amount.shape

    def layer(k, totals):
        totals = list(totals)
        for r in range(0, ly, 8):
            for c in range(0, lx, 128):
                at = (k, slice(r, r + 8), slice(c, c + 128))
                a, low, high = amount[at], low_v[at], high_v[at]
                if scale is not None:
                    a = a * scale
                for j, factor in enumerate(factors):
                    totals[j] = totals[j] + jnp.minimum(jnp.maximum(a * factor, low), high)
        return tuple(totals)

    totals = lax.fori_loop(0, lz, layer, tuple(jnp.zeros((8, 128), F32) for _ in factors))
    return to_lanes(totals, lanes)


def count_above(row, inside, target):
    return jnp.sum(jnp.where(inside & (row > target), 1.0, 0.0), axis=1, keepdims=True)


def entry(row, index):
    at = iota(row.shape, 1).astype(F32)
    return jnp.sum(jnp.where(at == index, row, 0.0), axis=1, keepdims=True)


def secant(low, low_volume, high_volume, target):
    return low + FINE * ((low_volume - target) / (low_volume - high_volume))


def weights(ref, z_ref, gy, ny, gz, nz):
    ly, lx = ref.shape
    lz = z_ref.shape[0]
    ref[...] = line_spread(iota((ly, lx), 0) + gy * ly, ly * ny) * line_spread(iota((ly, lx), 1), lx)
    z_ref[...] = line_spread(iota((lz, lx), 0) + gz * lz, lz * nz)


def bounds(weight, d, solid, void):
    low = jnp.maximum(d - MOVE_LIMIT, 0.0) * weight
    high = jnp.minimum(d + MOVE_LIMIT, 1.0) * weight
    is_solid, is_void = solid == 1, void == 1
    low = jnp.where(is_solid, weight, jnp.where(is_void, 0.0, low))
    high = jnp.where(is_solid, weight, jnp.where(is_void, 0.0, high))
    return low, high


def finished(a, weight, factor, d, solid, void):
    moved = (a / weight) * factor
    moved = jnp.minimum(
        jnp.maximum(moved, jnp.maximum(d - MOVE_LIMIT, 0.0)), jnp.minimum(d + MOVE_LIMIT, 1.0)
    )
    return jnp.where(solid == 1, 1.0, jnp.where(void == 1, 0.0, moved))


def total_target(lz, ly, lx, nz, ny):
    return VOLUME_FRACTION * (lz * nz) * (ly * ny) * lx


def kernel(
    nz, ny,
    disp, design, void, solid, stiff,
    new_design, sens, found,
    dpad, fpad, qpad, zbuf, void_v, solid_v, energy, amount, low_v, high_v, sens_v, new_v,
    tx, k_high, k_low, cube_yx, weight_yx, cube_z, weight_z, zs, qs, zq, sums,
    load_sem, store_sem, send1, recv1, send2, recv2, send_r, recv_r, known,
):
    lz, ly, lx = design.shape
    gz, gy = lax.axis_index("gz"), lax.axis_index("gy")
    has = {
        (1, 0): gz < nz - 1, (-1, 0): gz > 0, (0, 1): gy < ny - 1, (0, -1): gy > 0,
    }
    for dz in (-1, 1):
        for dy in (-1, 1):
            has[dz, dy] = has[dz, 0] & has[0, dy]

    def peer(dz, dy):
        return (lax.rem(gz + dz % nz, nz), lax.rem(gy + dy % ny, ny))

    directions = [(1, 0), (-1, 0), (0, 1), (0, -1), (1, 1), (1, -1), (-1, 1), (-1, -1)]

    own_f = fpad.at[H : H + lz, Y0 : Y0 + ly, :]
    loads = [
        pltpu.make_async_copy(disp, dpad.at[:, 0:lz, 0:ly, :], load_sem.at[0]),
        pltpu.make_async_copy(design, own_f, load_sem.at[1]),
        pltpu.make_async_copy(void, void_v, load_sem.at[2]),
        pltpu.make_async_copy(solid, solid_v, load_sem.at[3]),
    ]
    for copy in loads:
        copy.start()

    barrier = pltpu.get_barrier_semaphore()
    ways = directions + NEAR_Z + NEAR_Y
    for way in ways:
        pl.semaphore_signal(barrier, inc=1, device_id=peer(*way), device_id_type=MESH)

    tells = ((2, 0), (-2, 0), (0, 2), (0, -2))

    for pad in (fpad, qpad):
        @pl.when(gz == 0)
        def _():
            pad[0:H] = jnp.zeros_like(pad[0:H])

        @pl.when(gz == nz - 1)
        def _():
            pad[lz + H :] = jnp.zeros_like(pad[lz + H :])

        @pl.when(gy == 0)
        def _():
            pad[:, 0:Y0] = jnp.zeros_like(pad[:, 0:Y0])

        @pl.when(gy == ny - 1)
        def _():
            pad[:, Y0 + ly :] = jnp.zeros_like(pad[:, Y0 + ly :])

    @pl.when(gz == nz - 1)
    def _():
        dpad[:, lz] = jnp.zeros_like(dpad[:, lz])

    @pl.when(gy == ny - 1)
    def _():
        dpad[:, :, ly:] = jnp.zeros_like(dpad[:, :, ly:])

    pl.semaphore_wait(barrier, len(ways))
    for way in tells:
        pl.semaphore_signal(known, inc=1, device_id=peer(*way), device_id_type=MESH)

    near_z = {1: slice(lz - H, lz), -1: slice(0, H), 0: slice(0, lz)}
    near_y = {1: slice(ly - H, ly), -1: slice(0, H), 0: slice(0, ly)}
    far_z = {1: slice(0, H), -1: slice(H + lz, lz + 2 * H), 0: slice(H, H + lz)}
    far_y = {1: slice(Y0 - H, Y0), -1: slice(Y0 + ly, Y0 + ly + H), 0: slice(Y0, Y0 + ly)}

    def halo(src, src_at, pad, send, recv, n):
        dz, dy = directions[n]
        return pltpu.make_async_remote_copy(
            src_ref=src.at[src_at[0][dz], src_at[1][dy], :],
            dst_ref=pad.at[far_z[dz], far_y[dy], :],
            send_sem=send.at[n], recv_sem=recv.at[n],
            device_id=peer(dz, dy), device_id_type=MESH,
        )

    def start(direction, copy):
        @pl.when(has[direction])
        def _():
            copy.start()

    def wait_recv(direction, copy):
        @pl.when(has[-direction[0], -direction[1]])
        def _():
            copy.wait_recv()

    def wait_send(direction, copy):
        @pl.when(has[direction])
        def _():
            copy.wait_send()

    def nodes(n, direction, layers, rows, to_layers, to_rows):
        return direction, pltpu.make_async_remote_copy(
            src_ref=disp.at[:, layers, rows, :],
            dst_ref=dpad.at[:, to_layers, to_rows, :],
            send_sem=send1.at[8 + n], recv_sem=recv1.at[8 + n],
            device_id=peer(*direction), device_id_type=MESH,
        )

    first_z, top_z = slice(0, 1), slice(lz, lz + 1)
    first_y, top_y = slice(0, 1), slice(ly, ly + 1)
    own_z, own_y = slice(0, lz), slice(0, ly)
    node_copies = [
        nodes(0, (0, -1), own_z, first_y, own_z, top_y),
        nodes(1, (-1, -1), first_z, first_y, top_z, top_y),
        nodes(2, (-1, 0), first_z, own_y, top_z, own_y),
    ]
    design_copies = [
        (directions[n], halo(design, (near_z, near_y), fpad, send1, recv1, n)) for n in range(8)
    ]
    start(*design_copies[0])
    start(*design_copies[1])
    start(*node_copies[0])
    start(*node_copies[1])
    for n in range(2, 8):
        start(*design_copies[n])

    across = jnp.abs(iota((lx, lx), 0) - iota((lx, lx), 1))
    tx[...] = jnp.maximum(4 - across, 0).astype(F32).astype(BF16)
    full_z, full_y = lz * nz, ly * ny
    row_at = iota((ly, lx), 0) + gy * ly
    col_at = iota((ly, lx), 1)
    inv_yx = 1.0 / (line_total(row_at, full_y) * line_total(col_at, lx))
    cube_yx[...] = (-PENALTY) * inv_yx * inv_yx * inv_yx
    layer_at = iota((lz, lx), 0) + gz * lz
    inv_z = 1.0 / line_total(layer_at, full_z)
    cube_z[...] = inv_z * inv_z * inv_z
    weights(weight_yx, weight_z, gy, ny, gz, nz)

    size = 24 * 8
    pick = (lax.shift_right_logical(iota((size, 24), 0), 3) == iota((size, 24), 1)).astype(F32).astype(BF16)
    pick_t = (iota((24, size), 0) == lax.shift_right_logical(iota((24, size), 1), 3)).astype(F32).astype(BF16)
    same = (iota((size, size), 0) & 7) == (iota((size, size), 1) & 7)
    for part, ref in zip(split_bf16(stiff[...]), (k_high, k_low)):
        spread_k = dot(dot(pick, part).astype(BF16), pick_t)
        ref[...] = jnp.where(same, spread_k, 0.0).astype(BF16)

    last_col = iota((8, lx), 1) == lx - 1

    def element_rows(k, tile):
        at = tile * 8
        u = []
        for a in range(2):
            for b in range(2):
                here = [dpad[q, k + a, pl.ds(at + b, 8), :] for q in range(3)]
                u += here
                u += [jnp.where(last_col, 0.0, pltpu.roll(v, lx - 1, 1)) for v in here]
        u = jnp.concatenate(u, axis=0)
        high = u.astype(BF16)
        forces = dot(k_high[...], high) + dot(k_low[...], high)
        terms = (2.0 * u - high.astype(F32)) * forces
        total = jnp.sum(terms.reshape(24, 8, lx), axis=0)
        energy[k, pl.ds(at, 8), :] = jnp.maximum(total, 0.0)

    tiles = ly // 8

    def energy_of(count, layer_of, tiles_of):
        def body(n, carry):
            for k in layer_of(n):
                for tile in tiles_of:
                    element_rows(k, tile)
            return carry

        lax.fori_loop(0, count, body, 0)

    inner = lz - 2 * H
    sums_z, sums_y = lambda d: peer(d, 0), lambda d: peer(0, d)
    target = total_target(lz, ly, lx, nz, ny)
    lane = iota((1, 128), 1)

    def weight_of(k):
        return weight_yx[...] * weight_z[pl.ds(k, 1), :]

    s_z, s_y = lz // 2 - 1, ly // 2 - 4
    q_z, q_y = s_z - H, s_y - 4
    for load in loads:
        load.wait()
    energy_of(4, lambda n: [q_z + 2 * n, q_z + 2 * n + 1], [q_y // 8, q_y // 8 + 1])
    start(*node_copies[2])
    layer_filter(fpad, zs, 8, H + q_z - H, ly, Y0)
    f = jnp.concatenate([row_filter(zs, k, 16, q_y - Y0) for k in range(8)], axis=0)
    high, low = split_bf16(f)
    f = dot(high, tx[...]) + dot(low, tx[...])
    f = jnp.concatenate(
        [
            f[16 * k : 16 * k + 16] * f[16 * k : 16 * k + 16]
            * (energy[q_z + k, q_y : q_y + 16] * (cube_yx[q_y : q_y + 16] * cube_z[q_z + k : q_z + k + 1]))
            for k in range(8)
        ],
        axis=0,
    )
    high, low = split_bf16(f)
    f = dot(high, tx[...]) + dot(low, tx[...])
    for k in range(8):
        qs[k] = f[16 * k : 16 * k + 16]
    layer_filter(qs, zq, 2)
    sample = []
    for k in range(2):
        rows = slice(s_y, s_y + 8)
        d = fpad[H + s_z + k, Y0 + s_y : Y0 + s_y + 8]
        weight = weight_yx[rows] * weight_z[s_z + k : s_z + k + 1]
        a = d * jnp.sqrt(-row_filter(zq, k, 8, 4 - (Y0)) * weight)
        lo, hi = bounds(weight, d, solid_v[s_z + k, rows], void_v[s_z + k, rows])
        for c in range(0, lx, 128):
            sample.append((a[:, c : c + 128], lo[:, c : c + 128], hi[:, c : c + 128]))
    rough = (HIGH_LOG - LOW_LOG) / ROUGH
    totals = []
    for j in range(ROUGH):
        factor = E ** (-0.5 * (LOW_LOG + rough * j))
        parts = [jnp.minimum(jnp.maximum(a * factor, lo), hi) for a, lo, hi in sample]
        total = parts[0]
        for part in parts[1:]:
            total = total + part
        totals.append(total)
    row = to_lanes(totals, range(ROUGH))
    pl.semaphore_wait(known, len(tells))
    sum_start(0, row, gz, nz, sums_z, sums, send_r, recv_r)

    energy_of(2 * H - 1, lambda n: [n + (n // H) * inner], range(tiles - 1))
    rest = [k for k in range(H, lz - H) if not q_z <= k < q_z + 8]
    others = [t for t in range(1, tiles - 1) if not q_y // 8 <= t < q_y // 8 + 2]
    energy_of(1, lambda n: rest, range(1, tiles - 1))
    if others:
        energy_of(8, lambda n: [q_z + n], others)
    energy_of(inner // 2, lambda n: [H + 2 * n, H + 2 * n + 1], [0])
    wait_recv(*node_copies[0])
    wait_recv(*node_copies[1])
    energy_of((lz - 1) // 3, lambda n: [3 * n, 3 * n + 1, 3 * n + 2], [tiles - 1])

    for copy in design_copies:
        wait_recv(*copy)
    layer_filter(fpad, zbuf, lz)

    def source(layers, first, last):
        n = last - first
        f = jnp.concatenate([row_filter(zbuf, k, n, first) for k in layers], axis=0)
        high, low = split_bf16(f)
        f = dot(high, tx[...]) + dot(low, tx[...])
        cube = cube_yx[first:last]
        f = jnp.concatenate(
            [
                f[i * n : (i + 1) * n] * f[i * n : (i + 1) * n]
                * (energy[k, first:last] * (cube * cube_z[k : k + 1, :]))
                for i, k in enumerate(layers)
            ],
            axis=0,
        )
        high, low = split_bf16(f)
        f = dot(high, tx[...]) + dot(low, tx[...])
        for i, k in enumerate(layers):
            qpad[H + k, Y0 + first : Y0 + last, :] = f[i * n : (i + 1) * n]

    own_zq = {1: slice(lz, lz + H), -1: slice(H, 2 * H), 0: slice(H, H + lz)}
    own_yq = {1: slice(Y0 + ly - H, Y0 + ly), -1: slice(Y0, Y0 + H), 0: slice(Y0, Y0 + ly)}
    source_copies = [
        (directions[n], halo(qpad, (own_zq, own_yq), qpad, send2, recv2, n)) for n in range(8)
    ]
    source(range(H), 0, ly)
    start(*source_copies[1])
    start(*source_copies[6])
    start(*source_copies[7])
    wait_recv(*node_copies[2])
    for tile in range(tiles):
        element_rows(lz - 1, tile)
    source(range(lz - H, lz), 0, ly)
    start(*source_copies[0])
    start(*source_copies[4])
    start(*source_copies[5])
    middle = range(H, lz - H)
    source(middle, 0, 8)
    start(*source_copies[3])
    source(middle, ly - 8, ly)
    start(*source_copies[2])
    source(range(H, lz // 2), 8, ly - 8)
    source(range(lz // 2, lz - H), 8, ly - 8)

    def bounds_of(k, carry):
        low_v[k], high_v[k] = bounds(weight_of(k), fpad[H + k, Y0 : Y0 + ly, :], solid_v[k], void_v[k])
        return carry

    lax.fori_loop(0, lz, bounds_of, 0)

    row = sum_finish(0, nz, sums, recv_r)
    sum_start(1, row, gy, ny, sums_y, sums, send_r, recv_r)

    for copy in source_copies:
        wait_recv(*copy)
    layer_filter(qpad, zbuf, lz)
    for k in range(lz):
        s = row_filter(zbuf, k, ly)
        sens_v[k] = s
        amount[k] = fpad[H + k, Y0 : Y0 + ly, :] * jnp.sqrt(-s * weight_of(k))
    store_sens = pltpu.make_async_copy(sens_v, sens, store_sem.at[0])
    store_sens.start()

    row = sum_finish(1, ny, sums, recv_r)
    part = target * (16.0 / (lz * ly))
    index = count_above(row, lane < ROUGH, part)
    below, above = entry(row, index - 1.0), entry(row, index)
    step = jnp.where((index > 0.0) & (index < ROUGH), (below - part) / (below - above), 0.0)
    guess = (GRID // ROUGH) * (index - 1.0 + step)
    first = jnp.clip(jnp.floor(guess) - (WINDOW // 2 - 1), 0.0, GRID + 1.0 - WINDOW)
    low = LOW_LOG + FINE * first
    factors = [E ** (-0.5 * FINE * j) for j in range(WINDOW)]
    row = volumes(amount, low_v, high_v, jnp.exp(-0.5 * low), factors, range(WINDOW))
    sum_start(2, row, gz, nz, sums_z, sums, send_r, recv_r)
    row = sum_finish(2, nz, sums, recv_r)
    sum_start(3, row, gy, ny, sums_y, sums, send_r, recv_r)
    row = sum_finish(3, ny, sums, recv_r)
    index = count_above(row, lane < WINDOW, target)
    hit = (index > 0.0) & (index < WINDOW)
    found[...] = jnp.broadcast_to(jnp.where(hit, 1.0, 0.0), found.shape)
    index = index - 1.0
    final = secant(low + FINE * index, entry(row, index), entry(row, index + 1.0), target)
    factor = jnp.exp(-0.5 * final)

    def finish(k, carry):
        d = fpad[H + k, Y0 : Y0 + ly, :]
        new_v[k] = finished(amount[k], weight_of(k), factor, d, solid_v[k], void_v[k])
        return carry

    lax.fori_loop(0, lz, finish, 0)
    store_new = pltpu.make_async_copy(new_v, new_design, store_sem.at[1])
    store_new.start()

    for copy in node_copies + design_copies + source_copies:
        wait_send(*copy)
    for n, size in enumerate((nz, ny, nz, ny)):
        sum_sent(n, size, sums, send_r)
    store_sens.wait()
    store_new.wait()


def exact_kernel(
    nz, ny,
    design, void, solid, sens,
    new_design,
    design_v, void_v, solid_v, amount, low_v, high_v, new_v, weight_yx, weight_z, sums,
    load_sem, store_sem, send_r, recv_r,
):
    lz, ly, lx = design.shape
    gz, gy = lax.axis_index("gz"), lax.axis_index("gy")

    def sums_z(d):
        return (lax.rem(gz + d, nz), gy)

    def sums_y(d):
        return (gz, lax.rem(gy + d, ny))

    loads = [
        pltpu.make_async_copy(src, dst, load_sem.at[n])
        for n, (src, dst) in enumerate(
            ((design, design_v), (void, void_v), (solid, solid_v), (sens, amount))
        )
    ]
    for load in loads:
        load.start()
    barrier = pltpu.get_barrier_semaphore()
    partners = [sums_z(d) for d in range(1, nz)] + [sums_y(d) for d in range(1, ny)]
    for partner in partners:
        pl.semaphore_signal(barrier, inc=1, device_id=partner, device_id_type=MESH)
    weights(weight_yx, weight_z, gy, ny, gz, nz)
    for load in loads:
        load.wait()

    def weight_of(k):
        return weight_yx[...] * weight_z[pl.ds(k, 1), :]

    def prepare(k, carry):
        d = design_v[k]
        low_v[k], high_v[k] = bounds(weight_of(k), d, solid_v[k], void_v[k])
        amount[k] = d * jnp.sqrt(-amount[k] * weight_of(k))
        return carry

    lax.fori_loop(0, lz, prepare, 0)
    pl.semaphore_wait(barrier, len(partners))

    def everywhere(n, row):
        sum_start(n, row, gz, nz, sums_z, sums, send_r, recv_r)
        row = sum_finish(n, nz, sums, recv_r)
        sum_start(n + 1, row, gy, ny, sums_y, sums, send_r, recv_r)
        return sum_finish(n + 1, ny, sums, recv_r)

    target = total_target(lz, ly, lx, nz, ny)
    lane = iota((1, 128), 1)
    inside = (lane >= 1) & (lane < SPLIT)
    wide = FINE * SPLIT
    factors = [E ** (-0.5 * (LOW_LOG + wide * j)) for j in range(SPLIT + 1)]
    row = everywhere(0, volumes(amount, low_v, high_v, None, factors, range(SPLIT + 1)))
    index = count_above(row, inside, target)
    low = LOW_LOG + wide * index
    ends = (entry(row, index), entry(row, index + 1.0))
    factors = [E ** (-0.5 * FINE * j) for j in range(1, SPLIT)]
    row = everywhere(
        2, volumes(amount, low_v, high_v, jnp.exp(-0.5 * low), factors, range(1, SPLIT))
    )
    row = jnp.where(lane == 0, ends[0], jnp.where(lane == SPLIT, ends[1], row))
    index = count_above(row, inside, target)
    final = secant(low + FINE * index, entry(row, index), entry(row, index + 1.0), target)
    factor = jnp.exp(-0.5 * final)

    def finish(k, carry):
        new_v[k] = finished(amount[k], weight_of(k), factor, design_v[k], solid_v[k], void_v[k])
        return carry

    lax.fori_loop(0, lz, finish, 0)
    store = pltpu.make_async_copy(new_v, new_design, store_sem)
    store.start()
    for n, size in enumerate((nz, ny, nz, ny)):
        sum_sent(n, size, sums, send_r)
    store.wait()


def per_device(displacement, design, void_mask, solid_mask, stiffness):
    nz, ny = lax.axis_size("gz"), lax.axis_size("gy")
    lz, ly, lx = design.shape
    brick = jax.ShapeDtypeStruct(design.shape, F32)
    padded = (lz + 2 * H, ly + 16, lx)
    anywhere = pl.BlockSpec(memory_space=pltpu.HBM)
    sem = pltpu.SemaphoreType
    line, table = pltpu.VMEM((lz, lx), F32), pltpu.VMEM((ly, lx), F32)
    bricks = [pltpu.VMEM(design.shape, F32)] * 4
    masks = [pltpu.VMEM(design.shape, jnp.int32)] * 2
    sums = pltpu.VMEM((4, max(nz, ny), 1, 128), F32)
    new_design, sens, found = pl.pallas_call(
        functools.partial(kernel, nz, ny),
        out_shape=(brick, brick, jax.ShapeDtypeStruct((8, 128), F32)),
        in_specs=[anywhere] * 4 + [pl.BlockSpec(memory_space=pltpu.VMEM)],
        out_specs=(anywhere, anywhere, pl.BlockSpec(memory_space=pltpu.VMEM)),
        scratch_shapes=[
            pltpu.VMEM((3, lz + 1, ly + 8, lx), F32),
            pltpu.VMEM(padded, F32),
            pltpu.VMEM(padded, F32),
            pltpu.VMEM((lz, ly + 16, lx), F32),
            *masks,
            *bricks,
            pltpu.VMEM(design.shape, F32),
            pltpu.VMEM(design.shape, F32),
            pltpu.VMEM((lx, lx), BF16),
            pltpu.VMEM((192, 192), BF16),
            pltpu.VMEM((192, 192), BF16),
            table, table, line, line,
            pltpu.VMEM((8, ly, lx), F32),
            pltpu.VMEM((8, 16, lx), F32),
            pltpu.VMEM((2, 16, lx), F32),
            sums,
            sem.DMA((4,)), sem.DMA((2,)),
            sem.DMA((11,)), sem.DMA((11,)), sem.DMA((8,)), sem.DMA((8,)),
            sem.DMA((4,)), sem.DMA((4,)), sem.REGULAR,
        ],
        compiler_params=pltpu.CompilerParams(
            collective_id=0, has_side_effects=True, vmem_limit_bytes=60 * 1024 * 1024
        ),
    )(displacement, design, void_mask, solid_mask, stiffness)

    def exact(new_design, design, void_mask, solid_mask, sens):
        return pl.pallas_call(
            functools.partial(exact_kernel, nz, ny),
            out_shape=brick,
            in_specs=[anywhere] * 4,
            out_specs=anywhere,
            scratch_shapes=[
                pltpu.VMEM(design.shape, F32), *masks,
                *bricks,
                table, line, sums,
                sem.DMA((4,)), sem.DMA, sem.DMA((4,)), sem.DMA((4,)),
            ],
            compiler_params=pltpu.CompilerParams(
                collective_id=1, has_side_effects=True, vmem_limit_bytes=60 * 1024 * 1024
            ),
        )(design, void_mask, solid_mask, sens)

    new_design = lax.cond(
        found[0, 0] > 0.5, lambda new_design, *rest: new_design, exact,
        new_design, design, void_mask, solid_mask, sens,
    )
    return new_design, sens


def solution(mesh):
    return jax.shard_map(
        per_device,
        mesh=mesh,
        in_specs=(
            P(None, "gz", "gy", None),
            P("gz", "gy", None),
            P("gz", "gy", None),
            P("gz", "gy", None),
            P(),
        ),
        out_specs=(P("gz", "gy", None), P("gz", "gy", None)),
        check_vma=False,
    )
```

time: 56.4 us -> 47.9 us (0.85)
  Pallas kernels: 51.8 us -> 43.5 us
  local copies, waits for them, and re-layouts: 3.76 us -> 2.8 us
  between operations: 0.64 us -> 1.35 us
    pallas_call x1, Pallas kernels: 51.8 us -> 43.5 us  [per_device(): pl.pallas_call(functools.partial(kernel, nz, ny), out_shape=(brick, brick...]
    unnamed x2 -> x8, local copies, waits for them, and re-layouts: 3.76 us -> 1.6 us
    slice x0 -> x1, local copies, waits for them, and re-layouts: none -> 1.2 us  [per_device(): found[0, 0] > 0.5]
where the time goes in v3:
time: 47.9 us; the launch traced here: 47.7 us
  Pallas kernels  43.5 us (91%)
  local copies, waits for them, and re-layouts  2.8 us (6%)
  between operations  1.35 us (3%)
    pallas_call x1, Pallas kernels, per_device(): pl.pallas_call(functools.partial(kernel, nz, ny), out_shape=(brick, brick...  43.5 us
    unnamed x8, local copies, waits for them, and re-layouts  1.6 us
    slice x1, local copies, waits for them, and re-layouts, per_device(): found[0, 0] > 0.5  1.2 us

profile of v3, /device:TPU:1, one launch (start us, length us, event | category | flops | bytes accessed | tf_op | source)
XLA Modules:
  0.0 47.7 jit_solution(7449533690790511534)
XLA Ops:
  0.6 0.0 copy-start.2
  0.6 0.0 copy-start.1
  0.7 0.0 copy-start
  0.7 43.5 %shard_map.68 = (f32[16,32,256]{2,1,0:T(8,128)S(1)}, f32[16,32,256]{2,1,0:T(8,128)S(1)}, f32[8,128]{1,0:T(8,128)}) custom-call(f32[3,16,32,256]{3,2,1,0:T(8,128)} %disp.1, f32[16,32,256]{2,1,0:T(8,128)} %design.1, s32[16,32,256]{2,1,0:T(8,128)} %void.1, s32[16,32,256]{2,1,0:T(8,128)} %solid.1, f32[24,24]{1,0:T(8,128)} %stiff.1), custom_call_target="tpu_custom_call" | custom-call | tf_op jit(solution)/shard_map/pallas_call | solution.py:610
  44.2 1.2 %slice.3 = f32[1,1]{1,0:T(1,128)} slice(f32[8,128]{1,0:T(8,128)} %get-tuple-element.21), slice={[0:1], [0:1]} | slice | bytes 8 | tf_op jit(solution)/shard_map/slice | solution.py:659
  46.0 0.0 copy-done.2
  46.1 0.0 copy-done.1
  46.1 0.0 copy-done
  46.1 0.8 %copy.11 = f32[16,32,256]{2,1,0:T(8,128)} copy(f32[16,32,256]{2,1,0:T(8,128)S(1)} %get-tuple-element.28) | data formatting | bytes 1048576
  46.9 0.8 %copy.12 = f32[16,32,256]{2,1,0:T(8,128)} copy(f32[16,32,256]{2,1,0:T(8,128)S(1)} %get-tuple-element.27) | data formatting | bytes 1048576
  (1 shorter events, 0.0 us)
Async XLA Ops:
  0.6 45.4 %copy-start.2 = (s32[16,32,256]{2,1,0:T(8,128)S(1)}, s32[16,32,256]{2,1,0:T(8,128)}, u32[]{:S(2)}) copy-start(s32[16,32,256]{2,1,0:T(8,128)} %solid.1) | copy-start | bytes 1572868
  0.6 45.4 %copy-start.1 = (s32[16,32,256]{2,1,0:T(8,128)S(1)}, s32[16,32,256]{2,1,0:T(8,128)}, u32[]{:S(2)}) copy-start(s32[16,32,256]{2,1,0:T(8,128)} %void.1) | copy-start | bytes 1572868
  0.7 45.4 %copy-start = (f32[16,32,256]{2,1,0:T(8,128)S(1)}, f32[16,32,256]{2,1,0:T(8,128)}, u32[]{:S(2)}) copy-start(f32[16,32,256]{2,1,0:T(8,128)} %design.1) | copy-start | bytes 1572868

commit v4 on v3

--- a/solution.py
+++ b/solution.py
@@ -182,7 +182,7 @@
     disp, design, void, solid, stiff,
     new_design, sens, found,
     dpad, fpad, qpad, zbuf, void_v, solid_v, energy, amount, low_v, high_v, sens_v, new_v,
-    tx, k_high, k_low, cube_yx, weight_yx, cube_z, weight_z, zs, qs, zq, sums,
+    shifted, double, double_s, edge, tx, k_rows, cube_yx, weight_yx, cube_z, weight_z, zs, qs, zq, sums,
     load_sem, store_sem, send1, recv1, send2, recv2, send_r, recv_r, known,
 ):
     lz, ly, lx = design.shape
@@ -312,30 +312,64 @@
     cube_z[...] = inv_z * inv_z * inv_z
     weights(weight_yx, weight_z, gy, ny, gz, nz)
 
-    size = 24 * 8
+    size, width = 24 * 8, 12 * 8 + 16
     pick = (lax.shift_right_logical(iota((size, 24), 0), 3) == iota((size, 24), 1)).astype(F32).astype(BF16)
-    pick_t = (iota((24, size), 0) == lax.shift_right_logical(iota((24, size), 1), 3)).astype(F32).astype(BF16)
-    same = (iota((size, size), 0) & 7) == (iota((size, size), 1) & 7)
-    for part, ref in zip(split_bf16(stiff[...]), (k_high, k_low)):
-        spread_k = dot(dot(pick, part).astype(BF16), pick_t)
-        ref[...] = jnp.where(same, spread_k, 0.0).astype(BF16)
-
-    last_col = iota((8, lx), 1) == lx - 1
+    entry_at, col = iota((24, 2 * width), 0), iota((24, 2 * width), 1)
+
+    def part_col(col):
+        return jnp.where(col >= width, col - width, col)
+
+    col = part_col(col)
+    corner = sum((entry_at >= 6 * n).astype(jnp.int32) for n in (1, 2, 3))
+    step_y = corner & 1
+    rest = entry_at - 6 * corner
+    group = jnp.where(corner >= 2, 6, 0) + rest
+    tail = col - 12 * 8
+    tail_rest = tail & 7
+    tail_group = jnp.where(tail_rest < 6, jnp.where(tail >= 8, 6, 0) + tail_rest, -1)
+    col_group = jnp.where(col < 12 * 8, lax.shift_right_logical(col, 3), tail_group)
+    places = [
+        ((group == col_group) & (step_y == n)).astype(F32).astype(BF16) for n in range(2)
+    ]
+    col = part_col(iota((size, 2 * width), 1))
+    up = jnp.where(col < 12 * 8, col & 7, 8) - (iota((size, 2 * width), 0) & 7)
+    halves = []
+    for part in split_bf16(stiff[...]):
+        rows = dot(pick, part).astype(BF16)
+        same, next_row = dot(rows, places[0]), dot(rows, places[1])
+        halves.append(jnp.where(up == 0, same, jnp.where(up == 1, next_row, 0.0)))
+    is_low = iota((size, 2 * width), 1) >= width
+    k_rows[...] = jnp.where(is_low, halves[1], halves[0]).astype(BF16)
+
+    def nodes_at(k, first, last):
+        at = slice(first, last)
+        last_col = iota((last - first, lx), 1) == lx - 1
+        for q in range(3):
+            u = dpad[q, k, at]
+            v = jnp.where(last_col, 0.0, pltpu.roll(u, lx - 1, 1))
+            shifted[q, k, at] = v
+            double[q, k, at] = 2.0 * u - u.astype(BF16).astype(F32)
+            double_s[q, k, at] = 2.0 * v - v.astype(BF16).astype(F32)
+
+    def ninth_rows(k, tiles_of):
+        for tile in tiles_of:
+            at = slice(8 * tile + 8, 8 * tile + 9)
+            rows = [ref[q, k, at, :] for ref in (dpad, shifted) for q in range(3)]
+            edge[k, tile] = jnp.concatenate(rows + [jnp.zeros((2, lx), F32)], axis=0)
 
     def element_rows(k, tile):
-        at = tile * 8
-        u = []
-        for a in range(2):
-            for b in range(2):
-                here = [dpad[q, k + a, pl.ds(at + b, 8), :] for q in range(3)]
-                u += here
-                u += [jnp.where(last_col, 0.0, pltpu.roll(v, lx - 1, 1)) for v in here]
-        u = jnp.concatenate(u, axis=0)
-        high = u.astype(BF16)
-        forces = dot(k_high[...], high) + dot(k_low[...], high)
-        terms = (2.0 * u - high.astype(F32)) * forces
-        total = jnp.sum(terms.reshape(24, 8, lx), axis=0)
-        energy[k, pl.ds(at, 8), :] = jnp.maximum(total, 0.0)
+        at = slice(8 * tile, 8 * tile + 8)
+        u = [ref[q, k + a, at, :] for a in range(2) for ref in (dpad, shifted) for q in range(3)]
+        u += [edge[k + a, tile] for a in range(2)]
+        high = jnp.concatenate(u, axis=0).astype(BF16)
+        forces = dot(k_rows[...], jnp.concatenate([high, high], axis=0))
+        total = None
+        for n in range(24):
+            a, b, c, q = n // 12, n // 6 % 2, n // 3 % 2, n % 3
+            ref = double_s if c else double
+            term = ref[q, k + a, 8 * tile + b : 8 * tile + b + 8, :] * forces[8 * n : 8 * n + 8]
+            total = term if total is None else total + term
+        energy[k, at, :] = jnp.maximum(total, 0.0)
 
     tiles = ly // 8
 
@@ -360,6 +394,13 @@
     q_z, q_y = s_z - H, s_y - 4
     for load in loads:
         load.wait()
+
+    def own_nodes(k, carry):
+        nodes_at(k, 0, ly)
+        ninth_rows(k, range(tiles - 1))
+        return carry
+
+    lax.fori_loop(0, lz, own_nodes, 0)
     energy_of(4, lambda n: [q_z + 2 * n, q_z + 2 * n + 1], [q_y // 8, q_y // 8 + 1])
     start(*node_copies[2])
     layer_filter(fpad, zs, 8, H + q_z - H, ly, Y0)
@@ -410,6 +451,13 @@
     energy_of(inner // 2, lambda n: [H + 2 * n, H + 2 * n + 1], [0])
     wait_recv(*node_copies[0])
     wait_recv(*node_copies[1])
+
+    def side_nodes(k, carry):
+        nodes_at(k, ly, ly + 8)
+        ninth_rows(k, [tiles - 1])
+        return carry
+
+    lax.fori_loop(0, lz, side_nodes, 0)
     energy_of((lz - 1) // 3, lambda n: [3 * n, 3 * n + 1, 3 * n + 2], [tiles - 1])
 
     for copy in design_copies:
@@ -445,6 +493,8 @@
     start(*source_copies[6])
     start(*source_copies[7])
     wait_recv(*node_copies[2])
+    nodes_at(lz, 0, ly + 8)
+    ninth_rows(lz, range(tiles))
     for tile in range(tiles):
         element_rows(lz - 1, tile)
     source(range(lz - H, lz), 0, ly)
@@ -494,7 +544,7 @@
     row = sum_finish(3, ny, sums, recv_r)
     index = count_above(row, lane < WINDOW, target)
     hit = (index > 0.0) & (index < WINDOW)
-    found[...] = jnp.broadcast_to(jnp.where(hit, 1.0, 0.0), found.shape)
+    found[0] = jnp.sum(jnp.where(hit, 1.0, 0.0)).astype(jnp.int32)
     index = index - 1.0
     final = secant(low + FINE * index, entry(row, index), entry(row, index + 1.0), target)
     factor = jnp.exp(-0.5 * final)
@@ -596,6 +646,17 @@
     store.wait()
 
 
+def written_kernel(new_design, sens, new_out, sens_out, sem):
+    copies = [
+        pltpu.make_async_copy(src, dst, sem.at[n])
+        for n, (src, dst) in enumerate(((new_design, new_out), (sens, sens_out)))
+    ]
+    for copy in copies:
+        copy.start()
+    for copy in copies:
+        copy.wait()
+
+
 def per_device(displacement, design, void_mask, solid_mask, stiffness):
     nz, ny = lax.axis_size("gz"), lax.axis_size("gy")
     lz, ly, lx = design.shape
@@ -603,17 +664,18 @@
     padded = (lz + 2 * H, ly + 16, lx)
     anywhere = pl.BlockSpec(memory_space=pltpu.HBM)
     sem = pltpu.SemaphoreType
+    nodes = pltpu.VMEM((3, lz + 1, ly + 8, lx), F32)
     line, table = pltpu.VMEM((lz, lx), F32), pltpu.VMEM((ly, lx), F32)
     bricks = [pltpu.VMEM(design.shape, F32)] * 4
     masks = [pltpu.VMEM(design.shape, jnp.int32)] * 2
     sums = pltpu.VMEM((4, max(nz, ny), 1, 128), F32)
     new_design, sens, found = pl.pallas_call(
         functools.partial(kernel, nz, ny),
-        out_shape=(brick, brick, jax.ShapeDtypeStruct((8, 128), F32)),
+        out_shape=(brick, brick, jax.ShapeDtypeStruct((1,), jnp.int32)),
         in_specs=[anywhere] * 4 + [pl.BlockSpec(memory_space=pltpu.VMEM)],
-        out_specs=(anywhere, anywhere, pl.BlockSpec(memory_space=pltpu.VMEM)),
+        out_specs=(anywhere, anywhere, pl.BlockSpec(memory_space=pltpu.SMEM)),
         scratch_shapes=[
-            pltpu.VMEM((3, lz + 1, ly + 8, lx), F32),
+            nodes,
             pltpu.VMEM(padded, F32),
             pltpu.VMEM(padded, F32),
             pltpu.VMEM((lz, ly + 16, lx), F32),
@@ -621,9 +683,10 @@
             *bricks,
             pltpu.VMEM(design.shape, F32),
             pltpu.VMEM(design.shape, F32),
+            nodes, nodes, nodes,
+            pltpu.VMEM((lz + 1, ly // 8, 8, lx), F32),
             pltpu.VMEM((lx, lx), BF16),
-            pltpu.VMEM((192, 192), BF16),
-            pltpu.VMEM((192, 192), BF16),
+            pltpu.VMEM((192, 224), BF16),
             table, table, line, line,
             pltpu.VMEM((8, ly, lx), F32),
             pltpu.VMEM((8, 16, lx), F32),
@@ -655,11 +718,18 @@
             ),
         )(design, void_mask, solid_mask, sens)
 
-    new_design = lax.cond(
-        found[0, 0] > 0.5, lambda new_design, *rest: new_design, exact,
+    new_design = lax.switch(
+        found[0], (exact, lambda new_design, *rest: new_design),
         new_design, design, void_mask, solid_mask, sens,
     )
-    return new_design, sens
+    return pl.pallas_call(
+        written_kernel,
+        out_shape=(brick, brick),
+        in_specs=[anywhere] * 2,
+        out_specs=(anywhere, anywhere),
+        scratch_shapes=[sem.DMA((2,))],
+        compiler_params=pltpu.CompilerParams(vmem_limit_bytes=4 * 1024 * 1024),
+    )(new_design, sens)
 
 
 def solution(mesh):

time: 47.9 us -> 46.4 us (0.969)
  local copies, waits for them, and re-layouts: 2.8 us -> 0.01 us
  Pallas kernels: 43.5 us -> 45 us
    unnamed x8 -> x6, local copies, waits for them, and re-layouts: 1.6 us -> 0.01 us
    slice x1 -> x0, local copies, waits for them, and re-layouts: 1.2 us -> none  [per_device(): found[0, 0] > 0.5]
    pallas_call x0 -> x1, Pallas kernels: none -> 0.99 us  [per_device(): pl.pallas_call(written_kernel, out_shape=(brick, brick), in_specs=[anywhe...]
where the time goes in v4:
time: 46.4 us; the launch traced here: 46.2 us
  Pallas kernels  45 us (97%)
  between operations  1.25 us (3%)
    pallas_call x1, Pallas kernels, per_device(): pl.pallas_call(functools.partial(kernel, nz, ny), out_shape=(brick, brick...  44 us
    pallas_call x1, Pallas kernels, per_device(): pl.pallas_call(written_kernel, out_shape=(brick, brick), in_specs=[anywhe...  0.99 us

profile of v4, /device:TPU:1, one launch (start us, length us, event | category | flops | bytes accessed | tf_op | source)
XLA Modules:
  0.0 46.2 jit_solution(2927988280037477703)
XLA Ops:
  0.6 0.0 copy-start.2
  0.6 0.0 copy-start.1
  0.7 0.0 copy-start
  0.7 44.0 %shard_map.68 = (f32[16,32,256]{2,1,0:T(8,128)S(1)}, f32[16,32,256]{2,1,0:T(8,128)S(1)}, s32[1]{0:T(128)}) custom-call(f32[3,16,32,256]{3,2,1,0:T(8,128)} %disp.1, f32[16,32,256]{2,1,0:T(8,128)} %design.1, s32[16,32,256]{2,1,0:T(8,128)} %void.1, s32[16,32,256]{2,1,0:T(8,128)} %solid.1, f32[24,24]{1,0:T(8,128)} %stiff.1), custom_call_target="tpu_custom_call" | custom-call | tf_op jit(solution)/shard_map/pallas_call | solution.py:672
  45.2 0.0 copy-done.2
  45.2 0.0 copy-done.1
  45.2 0.0 copy-done
  45.3 1.0 %shard_map.69 = (f32[16,32,256]{2,1,0:T(8,128)}, f32[16,32,256]{2,1,0:T(8,128)}) custom-call(f32[16,32,256]{2,1,0:T(8,128)S(1)} %get-tuple-element.24.new_design, f32[16,32,256]{2,1,0:T(8,128)S(1)} %get-tuple-element.22.sens), custom_call_target="tpu_custom_call" | custom-call | tf_op jit(solution)/shard_map/pallas_call | solution.py:725
  (1 shorter events, 0.0 us)
Async XLA Ops:
  0.6 44.6 %copy-start.2 = (s32[16,32,256]{2,1,0:T(8,128)S(1)}, s32[16,32,256]{2,1,0:T(8,128)}, u32[]{:S(2)}) copy-start(s32[16,32,256]{2,1,0:T(8,128)} %solid.1) | copy-start | bytes 1572868
  0.6 44.6 %copy-start.1 = (s32[16,32,256]{2,1,0:T(8,128)S(1)}, s32[16,32,256]{2,1,0:T(8,128)}, u32[]{:S(2)}) copy-start(s32[16,32,256]{2,1,0:T(8,128)} %void.1) | copy-start | bytes 1572868
  0.7 44.6 %copy-start = (f32[16,32,256]{2,1,0:T(8,128)S(1)}, f32[16,32,256]{2,1,0:T(8,128)}, u32[]{:S(2)}) copy-start(f32[16,32,256]{2,1,0:T(8,128)} %design.1) | copy-start | bytes 1572868

commit v5 on v4

--- a/solution.py
+++ b/solution.py
@@ -8,8 +8,6 @@
 from jax.sharding import PartitionSpec as P
 
 MESH = pl.DeviceIdType.MESH
-NEAR_Z = [(d, 0) for d in (2, -2, 3, -3, 4, -4, 5, -5, 6, -6)]
-NEAR_Y = [(0, d) for d in (2, -2, 8, 7, 9, 6, 10)]
 F32 = jnp.float32
 BF16 = jnp.bfloat16
 
@@ -23,7 +21,7 @@
 GRID = SPLIT * SPLIT
 FINE = (HIGH_LOG - LOW_LOG) / GRID
 ROUGH = 64
-WINDOW = 14
+WINDOW = 8
 E = 2.718281828459045
 
 H = 3
@@ -183,7 +181,7 @@
     new_design, sens, found,
     dpad, fpad, qpad, zbuf, void_v, solid_v, energy, amount, low_v, high_v, sens_v, new_v,
     shifted, double, double_s, edge, tx, k_rows, cube_yx, weight_yx, cube_z, weight_z, zs, qs, zq, sums,
-    load_sem, store_sem, send1, recv1, send2, recv2, send_r, recv_r, known,
+    load_sem, store_sem, send1, recv1, send2, recv2, send_r, recv_r,
 ):
     lz, ly, lx = design.shape
     gz, gy = lax.axis_index("gz"), lax.axis_index("gy")
@@ -210,11 +208,9 @@
         copy.start()
 
     barrier = pltpu.get_barrier_semaphore()
-    ways = directions + NEAR_Z + NEAR_Y
+    ways = directions + [(d, 0) for d in range(2, nz - 1)] + [(0, d) for d in range(2, ny - 1)]
     for way in ways:
         pl.semaphore_signal(barrier, inc=1, device_id=peer(*way), device_id_type=MESH)
-
-    tells = ((2, 0), (-2, 0), (0, 2), (0, -2))
 
     for pad in (fpad, qpad):
         @pl.when(gz == 0)
@@ -242,8 +238,6 @@
         dpad[:, :, ly:] = jnp.zeros_like(dpad[:, :, ly:])
 
     pl.semaphore_wait(barrier, len(ways))
-    for way in tells:
-        pl.semaphore_signal(known, inc=1, device_id=peer(*way), device_id_type=MESH)
 
     near_z = {1: slice(lz - H, lz), -1: slice(0, H), 0: slice(0, lz)}
     near_y = {1: slice(ly - H, ly), -1: slice(0, H), 0: slice(0, ly)}
@@ -293,12 +287,12 @@
     design_copies = [
         (directions[n], halo(design, (near_z, near_y), fpad, send1, recv1, n)) for n in range(8)
     ]
+    for n in (4, 5, 6, 7, 2, 3):
+        start(*design_copies[n])
+    start(*node_copies[1])
+    start(*node_copies[0])
     start(*design_copies[0])
     start(*design_copies[1])
-    start(*node_copies[0])
-    start(*node_copies[1])
-    for n in range(2, 8):
-        start(*design_copies[n])
 
     across = jnp.abs(iota((lx, lx), 0) - iota((lx, lx), 1))
     tx[...] = jnp.maximum(4 - across, 0).astype(F32).astype(BF16)
@@ -439,7 +433,6 @@
             total = total + part
         totals.append(total)
     row = to_lanes(totals, range(ROUGH))
-    pl.semaphore_wait(known, len(tells))
     sum_start(0, row, gz, nz, sums_z, sums, send_r, recv_r)
 
     energy_of(2 * H - 1, lambda n: [n + (n // H) * inner], range(tiles - 1))
@@ -488,24 +481,21 @@
     source_copies = [
         (directions[n], halo(qpad, (own_zq, own_yq), qpad, send2, recv2, n)) for n in range(8)
     ]
+    middle = range(H, lz - H)
     source(range(H), 0, ly)
-    start(*source_copies[1])
-    start(*source_copies[6])
-    start(*source_copies[7])
+    source(middle, 0, 8)
+    source(middle, ly - 8, ly)
     wait_recv(*node_copies[2])
     nodes_at(lz, 0, ly + 8)
     ninth_rows(lz, range(tiles))
     for tile in range(tiles):
         element_rows(lz - 1, tile)
     source(range(lz - H, lz), 0, ly)
-    start(*source_copies[0])
-    start(*source_copies[4])
-    start(*source_copies[5])
-    middle = range(H, lz - H)
-    source(middle, 0, 8)
-    start(*source_copies[3])
-    source(middle, ly - 8, ly)
-    start(*source_copies[2])
+    for n in (4, 5, 6, 7, 2, 3, 0, 1):
+        start(*source_copies[n])
+    row = sum_finish(0, nz, sums, recv_r)
+    sum_start(1, row, gy, ny, sums_y, sums, send_r, recv_r)
+
     source(range(H, lz // 2), 8, ly - 8)
     source(range(lz // 2, lz - H), 8, ly - 8)
 
@@ -515,8 +505,16 @@
 
     lax.fori_loop(0, lz, bounds_of, 0)
 
-    row = sum_finish(0, nz, sums, recv_r)
-    sum_start(1, row, gy, ny, sums_y, sums, send_r, recv_r)
+    row = sum_finish(1, ny, sums, recv_r)
+    part = target * (16.0 / (lz * ly))
+    index = count_above(row, lane < ROUGH, part)
+    below, above = entry(row, index - 1.0), entry(row, index)
+    step = jnp.where((index > 0.0) & (index < ROUGH), (below - part) / (below - above), 0.0)
+    guess = (GRID // ROUGH) * (index - 1.0 + step)
+    first = jnp.clip(jnp.floor(guess) - (WINDOW // 2 - 1), 0.0, GRID + 1.0 - WINDOW)
+    low = LOW_LOG + FINE * first
+    window_factor = jnp.exp(-0.5 * low)
+    factors = [E ** (-0.5 * FINE * j) for j in range(WINDOW)]
 
     for copy in source_copies:
         wait_recv(*copy)
@@ -528,16 +526,7 @@
     store_sens = pltpu.make_async_copy(sens_v, sens, store_sem.at[0])
     store_sens.start()
 
-    row = sum_finish(1, ny, sums, recv_r)
-    part = target * (16.0 / (lz * ly))
-    index = count_above(row, lane < ROUGH, part)
-    below, above = entry(row, index - 1.0), entry(row, index)
-    step = jnp.where((index > 0.0) & (index < ROUGH), (below - part) / (below - above), 0.0)
-    guess = (GRID // ROUGH) * (index - 1.0 + step)
-    first = jnp.clip(jnp.floor(guess) - (WINDOW // 2 - 1), 0.0, GRID + 1.0 - WINDOW)
-    low = LOW_LOG + FINE * first
-    factors = [E ** (-0.5 * FINE * j) for j in range(WINDOW)]
-    row = volumes(amount, low_v, high_v, jnp.exp(-0.5 * low), factors, range(WINDOW))
+    row = volumes(amount, low_v, high_v, window_factor, factors, range(WINDOW))
     sum_start(2, row, gz, nz, sums_z, sums, send_r, recv_r)
     row = sum_finish(2, nz, sums, recv_r)
     sum_start(3, row, gy, ny, sums_y, sums, send_r, recv_r)
@@ -694,7 +683,7 @@
             sums,
             sem.DMA((4,)), sem.DMA((2,)),
             sem.DMA((11,)), sem.DMA((11,)), sem.DMA((8,)), sem.DMA((8,)),
-            sem.DMA((4,)), sem.DMA((4,)), sem.REGULAR,
+            sem.DMA((4,)), sem.DMA((4,)),
         ],
         compiler_params=pltpu.CompilerParams(
             collective_id=0, has_side_effects=True, vmem_limit_bytes=60 * 1024 * 1024

time: 46.4 us -> 47.9 us (1.032)
  Pallas kernels: 45 us -> 46.4 us
    pallas_call x1, Pallas kernels: 44 us -> 45.4 us  [per_device(): pl.pallas_call(functools.partial(kernel, nz, ny), out_shape=(brick, brick...]
where the time goes in v5:
time: 47.9 us; the launch traced here: 47.7 us
  Pallas kernels  46.4 us (97%)
  between operations  1.25 us (3%)
    pallas_call x1, Pallas kernels, per_device(): pl.pallas_call(functools.partial(kernel, nz, ny), out_shape=(brick, brick...  45.4 us
    pallas_call x1, Pallas kernels, per_device(): pl.pallas_call(written_kernel, out_shape=(brick, brick), in_specs=[anywhe...  0.99 us

profile of v5, /device:TPU:1, one launch (start us, length us, event | category | flops | bytes accessed | tf_op | source)
XLA Modules:
  0.0 47.7 jit_solution(6673864963290759720)
XLA Ops:
  0.6 0.0 copy-start.2
  0.6 0.0 copy-start.1
  0.7 0.0 copy-start
  0.7 45.4 %shard_map.68 = (f32[16,32,256]{2,1,0:T(8,128)S(1)}, f32[16,32,256]{2,1,0:T(8,128)S(1)}, s32[1]{0:T(128)}) custom-call(f32[3,16,32,256]{3,2,1,0:T(8,128)} %disp.1, f32[16,32,256]{2,1,0:T(8,128)} %design.1, s32[16,32,256]{2,1,0:T(8,128)} %void.1, s32[16,32,256]{2,1,0:T(8,128)} %solid.1, f32[24,24]{1,0:T(8,128)} %stiff.1), custom_call_target="tpu_custom_call" | custom-call | tf_op jit(solution)/shard_map/pallas_call | solution.py:661
  46.7 0.0 copy-done.2
  46.7 0.0 copy-done.1
  46.7 0.0 copy-done
  46.7 1.0 %shard_map.69 = (f32[16,32,256]{2,1,0:T(8,128)}, f32[16,32,256]{2,1,0:T(8,128)}) custom-call(f32[16,32,256]{2,1,0:T(8,128)S(1)} %get-tuple-element.24.new_design, f32[16,32,256]{2,1,0:T(8,128)S(1)} %get-tuple-element.22.sens), custom_call_target="tpu_custom_call" | custom-call | tf_op jit(solution)/shard_map/pallas_call | solution.py:714
  (1 shorter events, 0.0 us)
Async XLA Ops:
  0.6 46.0 %copy-start.2 = (s32[16,32,256]{2,1,0:T(8,128)S(1)}, s32[16,32,256]{2,1,0:T(8,128)}, u32[]{:S(2)}) copy-start(s32[16,32,256]{2,1,0:T(8,128)} %solid.1) | copy-start | bytes 1572868
  0.6 46.0 %copy-start.1 = (s32[16,32,256]{2,1,0:T(8,128)S(1)}, s32[16,32,256]{2,1,0:T(8,128)}, u32[]{:S(2)}) copy-start(s32[16,32,256]{2,1,0:T(8,128)} %void.1) | copy-start | bytes 1572868
  0.7 46.0 %copy-start = (f32[16,32,256]{2,1,0:T(8,128)S(1)}, f32[16,32,256]{2,1,0:T(8,128)}, u32[]{:S(2)}) copy-start(f32[16,32,256]{2,1,0:T(8,128)} %design.1) | copy-start | bytes 1572868

commit v6 on v4

--- a/solution.py
+++ b/solution.py
@@ -23,7 +23,7 @@
 GRID = SPLIT * SPLIT
 FINE = (HIGH_LOG - LOW_LOG) / GRID
 ROUGH = 64
-WINDOW = 14
+WINDOW = 8
 E = 2.718281828459045
 
 H = 3
@@ -68,18 +68,17 @@
     return (c[0] + c[6]) + 2.0 * (c[1] + c[5]) + 3.0 * (c[2] + c[4]) + 4.0 * c[3]
 
 
-def layer_filter(src, dst, layers, first=0, rows=None, first_row=0):
-    rows = src.shape[1] if rows is None else rows
-    for r in range(0, rows, 8):
+def layer_filter(src, dst, layers, first=0, rows=None, shift=0, to=0):
+    for r in range(0, src.shape[1], 8) if rows is None else rows:
         for c in range(0, src.shape[2], 128):
             col = slice(c, c + 128)
-            f = [src[first + k, first_row + r : first_row + r + 8, col] for k in range(layers + 2 * H)]
+            f = [src[first + k, shift + r : shift + r + 8, col] for k in range(layers + 2 * H)]
             f = [a + b for a, b in zip(f, f[1:])]
             f = [a + b for a, b in zip(f, f[2:])]
             f = [a + b for a, b in zip(f, f[1:])]
             f = [a + b for a, b in zip(f, f[2:])]
             for k in range(layers):
-                dst[k, r : r + 8, col] = f[k]
+                dst[to + k, r : r + 8, col] = f[k]
 
 
 def sum_start(n, row, at, size, to, sums, send, recv):
@@ -165,10 +164,9 @@
     return low, high
 
 
-def finished(a, weight, factor, d, solid, void):
-    moved = (a / weight) * factor
+def finished(b, factor, d, solid, void):
     moved = jnp.minimum(
-        jnp.maximum(moved, jnp.maximum(d - MOVE_LIMIT, 0.0)), jnp.minimum(d + MOVE_LIMIT, 1.0)
+        jnp.maximum(b * factor, jnp.maximum(d - MOVE_LIMIT, 0.0)), jnp.minimum(d + MOVE_LIMIT, 1.0)
     )
     return jnp.where(solid == 1, 1.0, jnp.where(void == 1, 0.0, moved))
 
@@ -180,9 +178,9 @@
 def kernel(
     nz, ny,
     disp, design, void, solid, stiff,
-    new_design, sens, found,
-    dpad, fpad, qpad, zbuf, void_v, solid_v, energy, amount, low_v, high_v, sens_v, new_v,
-    shifted, double, double_s, edge, tx, k_rows, cube_yx, weight_yx, cube_z, weight_z, zs, qs, zq, sums,
+    fields, found, factor_out,
+    dpad, fpad, qpad, zbuf, void_v, solid_v, energy, amount, scaled, low_v, high_v, sens_v,
+    shifted, double, double_s, edge, tx, stiff_v, k_rows, cube_yx, weight_yx, inv_yx, cube_z, weight_z, inv_z, zs, qs, zq, sums,
     load_sem, store_sem, send1, recv1, send2, recv2, send_r, recv_r, known,
 ):
     lz, ly, lx = design.shape
@@ -205,6 +203,7 @@
         pltpu.make_async_copy(design, own_f, load_sem.at[1]),
         pltpu.make_async_copy(void, void_v, load_sem.at[2]),
         pltpu.make_async_copy(solid, solid_v, load_sem.at[3]),
+        pltpu.make_async_copy(stiff, stiff_v, load_sem.at[4]),
     ]
     for copy in loads:
         copy.start()
@@ -293,24 +292,27 @@
     design_copies = [
         (directions[n], halo(design, (near_z, near_y), fpad, send1, recv1, n)) for n in range(8)
     ]
+    for n in (4, 5, 6, 7, 2, 3):
+        start(*design_copies[n])
+    start(*node_copies[1])
+    start(*node_copies[0])
     start(*design_copies[0])
     start(*design_copies[1])
-    start(*node_copies[0])
-    start(*node_copies[1])
-    for n in range(2, 8):
-        start(*design_copies[n])
+    start(*node_copies[2])
 
     across = jnp.abs(iota((lx, lx), 0) - iota((lx, lx), 1))
     tx[...] = jnp.maximum(4 - across, 0).astype(F32).astype(BF16)
     full_z, full_y = lz * nz, ly * ny
     row_at = iota((ly, lx), 0) + gy * ly
     col_at = iota((ly, lx), 1)
-    inv_yx = 1.0 / (line_total(row_at, full_y) * line_total(col_at, lx))
-    cube_yx[...] = (-PENALTY) * inv_yx * inv_yx * inv_yx
+    inv = 1.0 / (line_total(row_at, full_y) * line_total(col_at, lx))
+    cube_yx[...] = (-PENALTY) * inv * inv * inv
     layer_at = iota((lz, lx), 0) + gz * lz
-    inv_z = 1.0 / line_total(layer_at, full_z)
-    cube_z[...] = inv_z * inv_z * inv_z
+    inv = 1.0 / line_total(layer_at, full_z)
+    cube_z[...] = inv * inv * inv
     weights(weight_yx, weight_z, gy, ny, gz, nz)
+    inv_yx[...] = 1.0 / weight_yx[...]
+    inv_z[...] = 1.0 / weight_z[...]
 
     size, width = 24 * 8, 12 * 8 + 16
     pick = (lax.shift_right_logical(iota((size, 24), 0), 3) == iota((size, 24), 1)).astype(F32).astype(BF16)
@@ -334,7 +336,8 @@
     col = part_col(iota((size, 2 * width), 1))
     up = jnp.where(col < 12 * 8, col & 7, 8) - (iota((size, 2 * width), 0) & 7)
     halves = []
-    for part in split_bf16(stiff[...]):
+    loads[4].wait()
+    for part in split_bf16(stiff_v[...]):
         rows = dot(pick, part).astype(BF16)
         same, next_row = dot(rows, places[0]), dot(rows, places[1])
         halves.append(jnp.where(up == 0, same, jnp.where(up == 1, next_row, 0.0)))
@@ -392,7 +395,7 @@
 
     s_z, s_y = lz // 2 - 1, ly // 2 - 4
     q_z, q_y = s_z - H, s_y - 4
-    for load in loads:
+    for load in loads[:4]:
         load.wait()
 
     def own_nodes(k, carry):
@@ -402,8 +405,7 @@
 
     lax.fori_loop(0, lz, own_nodes, 0)
     energy_of(4, lambda n: [q_z + 2 * n, q_z + 2 * n + 1], [q_y // 8, q_y // 8 + 1])
-    start(*node_copies[2])
-    layer_filter(fpad, zs, 8, H + q_z - H, ly, Y0)
+    layer_filter(fpad, zs, 8, q_z, range(0, ly, 8), Y0)
     f = jnp.concatenate([row_filter(zs, k, 16, q_y - Y0) for k in range(8)], axis=0)
     high, low = split_bf16(f)
     f = dot(high, tx[...]) + dot(low, tx[...])
@@ -488,24 +490,21 @@
     source_copies = [
         (directions[n], halo(qpad, (own_zq, own_yq), qpad, send2, recv2, n)) for n in range(8)
     ]
+    middle = range(H, lz - H)
     source(range(H), 0, ly)
     start(*source_copies[1])
     start(*source_copies[6])
     start(*source_copies[7])
+    source(middle, 0, 8)
+    source(middle, ly - 8, ly)
     wait_recv(*node_copies[2])
     nodes_at(lz, 0, ly + 8)
     ninth_rows(lz, range(tiles))
     for tile in range(tiles):
         element_rows(lz - 1, tile)
     source(range(lz - H, lz), 0, ly)
-    start(*source_copies[0])
-    start(*source_copies[4])
-    start(*source_copies[5])
-    middle = range(H, lz - H)
-    source(middle, 0, 8)
-    start(*source_copies[3])
-    source(middle, ly - 8, ly)
-    start(*source_copies[2])
+    for n in (2, 3, 4, 5, 0):
+        start(*source_copies[n])
     source(range(H, lz // 2), 8, ly - 8)
     source(range(lz // 2, lz - H), 8, ly - 8)
 
@@ -517,16 +516,26 @@
 
     row = sum_finish(0, nz, sums, recv_r)
     sum_start(1, row, gy, ny, sums_y, sums, send_r, recv_r)
+
+    def finish_sens(k, first, last):
+        at = slice(first, last)
+        s = row_filter(zbuf, k, last - first, first)
+        sens_v[k, at] = s
+        b = fpad[H + k, Y0 + first : Y0 + last] * jnp.sqrt(-s * (inv_yx[at] * inv_z[k : k + 1]))
+        amount[k, at] = b
+        scaled[k, at] = b * (weight_yx[at] * weight_z[k : k + 1])
 
     for copy in source_copies:
         wait_recv(*copy)
     layer_filter(qpad, zbuf, lz)
     for k in range(lz):
-        s = row_filter(zbuf, k, ly)
-        sens_v[k] = s
-        amount[k] = fpad[H + k, Y0 : Y0 + ly, :] * jnp.sqrt(-s * weight_of(k))
-    store_sens = pltpu.make_async_copy(sens_v, sens, store_sem.at[0])
-    store_sens.start()
+        finish_sens(k, 0, ly)
+    stores = [
+        pltpu.make_async_copy(src, dst, store_sem.at[n])
+        for n, (src, dst) in enumerate(((sens_v, fields.at[0]), (amount, fields.at[1])))
+    ]
+    for store in stores:
+        store.start()
 
     row = sum_finish(1, ny, sums, recv_r)
     part = target * (16.0 / (lz * ly))
@@ -536,8 +545,9 @@
     guess = (GRID // ROUGH) * (index - 1.0 + step)
     first = jnp.clip(jnp.floor(guess) - (WINDOW // 2 - 1), 0.0, GRID + 1.0 - WINDOW)
     low = LOW_LOG + FINE * first
+    window_factor = jnp.exp(-0.5 * low)
     factors = [E ** (-0.5 * FINE * j) for j in range(WINDOW)]
-    row = volumes(amount, low_v, high_v, jnp.exp(-0.5 * low), factors, range(WINDOW))
+    row = volumes(scaled, low_v, high_v, window_factor, factors, range(WINDOW))
     sum_start(2, row, gz, nz, sums_z, sums, send_r, recv_r)
     row = sum_finish(2, nz, sums, recv_r)
     sum_start(3, row, gy, ny, sums_y, sums, send_r, recv_r)
@@ -549,29 +559,22 @@
     final = secant(low + FINE * index, entry(row, index), entry(row, index + 1.0), target)
     factor = jnp.exp(-0.5 * final)
 
-    def finish(k, carry):
-        d = fpad[H + k, Y0 : Y0 + ly, :]
-        new_v[k] = finished(amount[k], weight_of(k), factor, d, solid_v[k], void_v[k])
-        return carry
-
-    lax.fori_loop(0, lz, finish, 0)
-    store_new = pltpu.make_async_copy(new_v, new_design, store_sem.at[1])
-    store_new.start()
+    factor_out[0] = jnp.sum(factor)
 
     for copy in node_copies + design_copies + source_copies:
         wait_send(*copy)
     for n, size in enumerate((nz, ny, nz, ny)):
         sum_sent(n, size, sums, send_r)
-    store_sens.wait()
-    store_new.wait()
+    for store in stores:
+        store.wait()
 
 
 def exact_kernel(
     nz, ny,
-    design, void, solid, sens,
-    new_design,
-    design_v, void_v, solid_v, amount, low_v, high_v, new_v, weight_yx, weight_z, sums,
-    load_sem, store_sem, send_r, recv_r,
+    design, void, solid, fields,
+    factor_out,
+    design_v, void_v, solid_v, amount, low_v, high_v, weight_yx, weight_z, sums,
+    load_sem, send_r, recv_r,
 ):
     lz, ly, lx = design.shape
     gz, gy = lax.axis_index("gz"), lax.axis_index("gy")
@@ -585,7 +588,7 @@
     loads = [
         pltpu.make_async_copy(src, dst, load_sem.at[n])
         for n, (src, dst) in enumerate(
-            ((design, design_v), (void, void_v), (solid, solid_v), (sens, amount))
+            ((design, design_v), (void, void_v), (solid, solid_v), (fields.at[0], amount))
         )
     ]
     for load in loads:
@@ -634,27 +637,26 @@
     final = secant(low + FINE * index, entry(row, index), entry(row, index + 1.0), target)
     factor = jnp.exp(-0.5 * final)
 
-    def finish(k, carry):
-        new_v[k] = finished(amount[k], weight_of(k), factor, design_v[k], solid_v[k], void_v[k])
-        return carry
-
-    lax.fori_loop(0, lz, finish, 0)
-    store = pltpu.make_async_copy(new_v, new_design, store_sem)
-    store.start()
+    factor_out[0] = jnp.sum(factor)
     for n, size in enumerate((nz, ny, nz, ny)):
         sum_sent(n, size, sums, send_r)
-    store.wait()
-
-
-def written_kernel(new_design, sens, new_out, sens_out, sem):
-    copies = [
-        pltpu.make_async_copy(src, dst, sem.at[n])
-        for n, (src, dst) in enumerate(((new_design, new_out), (sens, sens_out)))
-    ]
-    for copy in copies:
-        copy.start()
-    for copy in copies:
-        copy.wait()
+
+
+def written_kernel(
+    factor, design, void, solid, fields, new_out, sens_out, new_v, store_sem, sens_sem
+):
+    parts, step = new_v.shape[0], new_v.shape[1]
+    copy_sens = pltpu.make_async_copy(fields.at[0], sens_out, sens_sem)
+    copy_sens.start()
+    stores = []
+    for n in range(parts):
+        at = slice(n * step, (n + 1) * step)
+        new_v[n] = finished(fields[1, at], factor[0], design[at], solid[at], void[at])
+        stores.append(pltpu.make_async_copy(new_v.at[n], new_out.at[at], store_sem.at[n]))
+        stores[n].start()
+    for store in stores:
+        store.wait()
+    copy_sens.wait()
 
 
 def per_device(displacement, design, void_mask, solid_mask, stiffness):
@@ -669,11 +671,15 @@
     bricks = [pltpu.VMEM(design.shape, F32)] * 4
     masks = [pltpu.VMEM(design.shape, jnp.int32)] * 2
     sums = pltpu.VMEM((4, max(nz, ny), 1, 128), F32)
-    new_design, sens, found = pl.pallas_call(
+    scalar = pl.BlockSpec(memory_space=pltpu.SMEM)
+    one = jax.ShapeDtypeStruct((1,), F32)
+    fields, found, factor = pl.pallas_call(
         functools.partial(kernel, nz, ny),
-        out_shape=(brick, brick, jax.ShapeDtypeStruct((1,), jnp.int32)),
-        in_specs=[anywhere] * 4 + [pl.BlockSpec(memory_space=pltpu.VMEM)],
-        out_specs=(anywhere, anywhere, pl.BlockSpec(memory_space=pltpu.SMEM)),
+        out_shape=(
+            jax.ShapeDtypeStruct((2, *design.shape), F32), jax.ShapeDtypeStruct((1,), jnp.int32), one
+        ),
+        in_specs=[anywhere] * 5,
+        out_specs=(anywhere, scalar, scalar),
         scratch_shapes=[
             nodes,
             pltpu.VMEM(padded, F32),
@@ -681,18 +687,18 @@
             pltpu.VMEM((lz, ly + 16, lx), F32),
             *masks,
             *bricks,
-            pltpu.VMEM(design.shape, F32),
-            pltpu.VMEM(design.shape, F32),
+            pltpu.VMEM(design.shape, F32), pltpu.VMEM(design.shape, F32),
             nodes, nodes, nodes,
             pltpu.VMEM((lz + 1, ly // 8, 8, lx), F32),
             pltpu.VMEM((lx, lx), BF16),
+            pltpu.VMEM((24, 24), F32),
             pltpu.VMEM((192, 224), BF16),
-            table, table, line, line,
+            table, table, table, line, line, line,
             pltpu.VMEM((8, ly, lx), F32),
             pltpu.VMEM((8, 16, lx), F32),
             pltpu.VMEM((2, 16, lx), F32),
             sums,
-            sem.DMA((4,)), sem.DMA((2,)),
+            sem.DMA((5,)), sem.DMA((2,)),
             sem.DMA((11,)), sem.DMA((11,)), sem.DMA((8,)), sem.DMA((8,)),
             sem.DMA((4,)), sem.DMA((4,)), sem.REGULAR,
         ],
@@ -701,35 +707,38 @@
         ),
     )(displacement, design, void_mask, solid_mask, stiffness)
 
-    def exact(new_design, design, void_mask, solid_mask, sens):
+    def exact(factor, design, void_mask, solid_mask, fields):
         return pl.pallas_call(
             functools.partial(exact_kernel, nz, ny),
-            out_shape=brick,
+            out_shape=one,
             in_specs=[anywhere] * 4,
-            out_specs=anywhere,
+            out_specs=scalar,
             scratch_shapes=[
                 pltpu.VMEM(design.shape, F32), *masks,
-                *bricks,
+                *bricks[:3],
                 table, line, sums,
-                sem.DMA((4,)), sem.DMA, sem.DMA((4,)), sem.DMA((4,)),
+                sem.DMA((4,)), sem.DMA((4,)), sem.DMA((4,)),
             ],
             compiler_params=pltpu.CompilerParams(
                 collective_id=1, has_side_effects=True, vmem_limit_bytes=60 * 1024 * 1024
             ),
-        )(design, void_mask, solid_mask, sens)
-
-    new_design = lax.switch(
-        found[0], (exact, lambda new_design, *rest: new_design),
-        new_design, design, void_mask, solid_mask, sens,
+        )(design, void_mask, solid_mask, fields)
+
+    factor = lax.switch(
+        found[0], (exact, lambda factor, *rest: factor),
+        factor, design, void_mask, solid_mask, fields,
     )
+    parts = 4
     return pl.pallas_call(
         written_kernel,
         out_shape=(brick, brick),
-        in_specs=[anywhere] * 2,
+        in_specs=[scalar] + [pl.BlockSpec(memory_space=pltpu.VMEM)] * 4,
         out_specs=(anywhere, anywhere),
-        scratch_shapes=[sem.DMA((2,))],
-        compiler_params=pltpu.CompilerParams(vmem_limit_bytes=4 * 1024 * 1024),
-    )(new_design, sens)
+        scratch_shapes=[
+            pltpu.VMEM((parts, lz // parts, ly, lx), F32), sem.DMA((parts,)), sem.DMA
+        ],
+        compiler_params=pltpu.CompilerParams(vmem_limit_bytes=16 * 1024 * 1024),
+    )(factor, design, void_mask, solid_mask, fields)
 
 
 def solution(mesh):

time: 46.4 us -> 45.3 us (0.976)
  Pallas kernels: 45 us -> 43.8 us
    pallas_call x2, Pallas kernels: 45 us -> 43.8 us  [the longest x1 42.2 us: per_device(): pl.pallas_call(functools.partial(kernel, nz, ny), out_shape=(jax.ShapeDty...]
where the time goes in v6:
time: 45.3 us; the launch traced here: 45.2 us
  Pallas kernels  43.8 us (97%)
  between operations  1.38 us (3%)
    pallas_call x1, Pallas kernels, per_device(): pl.pallas_call(functools.partial(kernel, nz, ny), out_shape=(jax.ShapeDty...  42.2 us
    pallas_call x1, Pallas kernels, per_device(): pl.pallas_call(written_kernel, out_shape=(brick, brick), in_specs=[scalar...  1.58 us

profile of v6, /device:TPU:1, one launch (start us, length us, event | category | flops | bytes accessed | tf_op | source)
XLA Modules:
  0.0 45.2 jit_solution(8358832511322808751)
XLA Ops:
  0.6 0.0 copy-start.2
  0.6 0.0 copy-start.1
  0.7 0.0 copy-start
  0.7 42.2 %shard_map.68 = (f32[2,16,32,256]{3,2,1,0:T(8,128)S(1)}, s32[1]{0:T(128)}, f32[1]{0:T(128)}) custom-call(f32[3,16,32,256]{3,2,1,0:T(8,128)} %disp.1, f32[16,32,256]{2,1,0:T(8,128)} %design.3, s32[16,32,256]{2,1,0:T(8,128)} %void.3, s32[16,32,256]{2,1,0:T(8,128)} %solid.3, f32[24,24]{1,0:T(8,128)} %stiff.1), custom_call_target="tpu_custom_call" | custom-call | tf_op jit(solution)/shard_map/pallas_call | solution.py:676
  43.6 0.0 copy-done.2
  43.6 0.0 copy-done.1
  43.6 0.0 copy-done
  43.6 1.6 %shard_map.69 = (f32[16,32,256]{2,1,0:T(8,128)}, f32[16,32,256]{2,1,0:T(8,128)}) custom-call(f32[1]{0:T(128)} %get-tuple-element.24.factor, f32[16,32,256]{2,1,0:T(8,128)S(1)} %copy-done, s32[16,32,256]{2,1,0:T(8,128)S(1)} %copy-done.1, s32[16,32,256]{2,1,0:T(8,128)S(1)} %copy-done.2, f32[2,16,32,256]{3,2,1,0:T(8,128)S(1)} %get-tuple-element.22.fields), custom_call_target="tpu_custom_call" | custom-call | tf_op jit(solution)/shard_map/pallas_call | solution.py:732
  (1 shorter events, 0.0 us)
Async XLA Ops:
  0.6 42.9 %copy-start.2 = (s32[16,32,256]{2,1,0:T(8,128)S(1)}, s32[16,32,256]{2,1,0:T(8,128)}, u32[]{:S(2)}) copy-start(s32[16,32,256]{2,1,0:T(8,128)} %solid.3) | copy-start | bytes 1572868
  0.6 42.9 %copy-start.1 = (s32[16,32,256]{2,1,0:T(8,128)S(1)}, s32[16,32,256]{2,1,0:T(8,128)}, u32[]{:S(2)}) copy-start(s32[16,32,256]{2,1,0:T(8,128)} %void.3) | copy-start | bytes 1572868
  0.7 42.9 %copy-start = (f32[16,32,256]{2,1,0:T(8,128)S(1)}, f32[16,32,256]{2,1,0:T(8,128)}, u32[]{:S(2)}) copy-start(f32[16,32,256]{2,1,0:T(8,128)} %design.3) | copy-start | bytes 1572868

commit v7 on v6

--- a/solution.py
+++ b/solution.py
@@ -23,7 +23,7 @@
 GRID = SPLIT * SPLIT
 FINE = (HIGH_LOG - LOW_LOG) / GRID
 ROUGH = 64
-WINDOW = 8
+WINDOW = 6
 E = 2.718281828459045
 
 H = 3
@@ -525,11 +525,21 @@
         amount[k, at] = b
         scaled[k, at] = b * (weight_yx[at] * weight_z[k : k + 1])
 
+    every = range(0, ly + 16, 8)
+    layer_filter(qpad, zbuf, inner, H, range(Y0, Y0 + ly, 8), 0, H)
+    for k in middle:
+        finish_sens(k, 8, ly - 8)
     for copy in source_copies:
         wait_recv(*copy)
-    layer_filter(qpad, zbuf, lz)
+    layer_filter(qpad, zbuf, H, 0, every)
+    layer_filter(qpad, zbuf, H, lz - H, every, 0, lz - H)
+    layer_filter(qpad, zbuf, inner, H, (0, Y0 + ly), 0, H)
     for k in range(lz):
-        finish_sens(k, 0, ly)
+        if k in middle:
+            finish_sens(k, 0, 8)
+            finish_sens(k, ly - 8, ly)
+        else:
+            finish_sens(k, 0, ly)
     stores = [
         pltpu.make_async_copy(src, dst, store_sem.at[n])
         for n, (src, dst) in enumerate(((sens_v, fields.at[0]), (amount, fields.at[1])))
@@ -728,7 +738,7 @@
         found[0], (exact, lambda factor, *rest: factor),
         factor, design, void_mask, solid_mask, fields,
     )
-    parts = 4
+    parts = 8
     return pl.pallas_call(
         written_kernel,
         out_shape=(brick, brick),

time: 45.3 us -> 45 us (level)
  no operation moved by 1% of the time
where the time goes in v7:
time: 45 us; the launch traced here: 44.9 us
  Pallas kernels  43.5 us (97%)
  between operations  1.38 us (3%)
    pallas_call x1, Pallas kernels, per_device(): pl.pallas_call(functools.partial(kernel, nz, ny), out_shape=(jax.ShapeDty...  41.9 us
    pallas_call x1, Pallas kernels, per_device(): pl.pallas_call(written_kernel, out_shape=(brick, brick), in_specs=[scalar...  1.62 us

profile of v7, /device:TPU:1, one launch (start us, length us, event | category | flops | bytes accessed | tf_op | source)
XLA Modules:
  0.0 44.9 jit_solution(18226763390461551201)
XLA Ops:
  0.6 0.0 copy-start.2
  0.6 0.0 copy-start.1
  0.7 0.0 copy-start
  0.7 41.9 %shard_map.68 = (f32[2,16,32,256]{3,2,1,0:T(8,128)S(1)}, s32[1]{0:T(128)}, f32[1]{0:T(128)}) custom-call(f32[3,16,32,256]{3,2,1,0:T(8,128)} %disp.1, f32[16,32,256]{2,1,0:T(8,128)} %design.3, s32[16,32,256]{2,1,0:T(8,128)} %void.3, s32[16,32,256]{2,1,0:T(8,128)} %solid.3, f32[24,24]{1,0:T(8,128)} %stiff.1), custom_call_target="tpu_custom_call" | custom-call | tf_op jit(solution)/shard_map/pallas_call | solution.py:686
  43.2 0.0 copy-done.2
  43.3 0.0 copy-done.1
  43.3 0.0 copy-done
  43.3 1.6 %shard_map.69 = (f32[16,32,256]{2,1,0:T(8,128)}, f32[16,32,256]{2,1,0:T(8,128)}) custom-call(f32[1]{0:T(128)} %get-tuple-element.24.factor, f32[16,32,256]{2,1,0:T(8,128)S(1)} %copy-done, s32[16,32,256]{2,1,0:T(8,128)S(1)} %copy-done.1, s32[16,32,256]{2,1,0:T(8,128)S(1)} %copy-done.2, f32[2,16,32,256]{3,2,1,0:T(8,128)S(1)} %get-tuple-element.22.fields), custom_call_target="tpu_custom_call" | custom-call | tf_op jit(solution)/shard_map/pallas_call | solution.py:742
  (1 shorter events, 0.0 us)
Async XLA Ops:
  0.6 42.6 %copy-start.2 = (s32[16,32,256]{2,1,0:T(8,128)S(1)}, s32[16,32,256]{2,1,0:T(8,128)}, u32[]{:S(2)}) copy-start(s32[16,32,256]{2,1,0:T(8,128)} %solid.3) | copy-start | bytes 1572868
  0.6 42.6 %copy-start.1 = (s32[16,32,256]{2,1,0:T(8,128)S(1)}, s32[16,32,256]{2,1,0:T(8,128)}, u32[]{:S(2)}) copy-start(s32[16,32,256]{2,1,0:T(8,128)} %void.3) | copy-start | bytes 1572868
  0.7 42.6 %copy-start = (f32[16,32,256]{2,1,0:T(8,128)S(1)}, f32[16,32,256]{2,1,0:T(8,128)}, u32[]{:S(2)}) copy-start(f32[16,32,256]{2,1,0:T(8,128)} %design.3) | copy-start | bytes 1572868
